TPU v7x, 32 devices: a whole 2x2x4 slice. The times are simulated.
32 devices in a mesh: section: 2 (over core), blk: 16 (over z, y, x).
Axes of the slice: x: 2, y: 2, z: 4, core: 2. Of those that a mesh axis runs over, the one named last changes fastest.
Arguments:
- hidden: bfloat16 [2, 48, 3072], P(None, 'blk'), may hold values from -4 to 4
- qkv_weight: bfloat16 [2, 3072, 9216], P('section', None, 'blk'), may hold values from -0.109375 to 0.109375
- out_weight: bfloat16 [2, 3072, 3072], P('section', None, 'blk'), may hold values from -0.109375 to 0.109375
- modulation: float32 [2, 50, 3, 3072], P('section'), may hold values from -3 to 3
- timestep: int32 [1], replicated, may hold values from 0 to 49
- fresh: int32 [2, 2, 16], P('section'), may hold values 0 or 1
- live: int32 [2, 16], replicated, may hold values from 0 to 1, as said below
- k_stale: bfloat16 [2, 2, 48, 3072], P('section', None, 'blk'), may hold values from -6 to 6
- v_stale: bfloat16 [2, 2, 48, 3072], P('section', None, 'blk'), may hold values from -16 to 16
Outputs:
- layer_outputs: bfloat16 [2, 2, 48, 3072], P('section', None, 'blk')
Inputs may be any that keep to these rules, and one draw needn't show every extreme that they name: Block 0 of every request is live.
All inputs are finite; a program needn't handle non-finite values. No bound on the sum of `fresh` on one device may be relied on, other than what follows from the above.
Results may differ from a plain program's by a relative error of at most 0.017.
Values may be sent and summed in bfloat16 or wider, within the bound.
No kernel may reach another device: no remote copies, remote signals or barrier semaphores. Data moves between devices by JAX's collectives and lax.ppermute only.
A program may use at most 64 MiB of HBM per device.

v0:
```python
import functools

import jax
import jax.numpy as jnp
from jax import lax
from jax.experimental import pallas as pl
from jax.experimental.pallas import tpu as pltpu
from jax.sharding import PartitionSpec as P


def from_behind(shard, axis, by):
    count = lax.axis_size(axis)
    pairs = [(i, i + by) for i in range(count) if 0 <= i + by < count]
    return lax.ppermute(shard, axis, pairs)


def attend(layer_in, qkv_cols, out_cols, modulate, fresh_own, old_keys, old_values, live):
    stream = layer_in.astype(jnp.float32)
    center = jnp.mean(stream, axis=-1, keepdims=True)
    variance = jnp.mean((stream - center) ** 2, axis=-1, keepdims=True)
    normed = (stream - center) / jnp.sqrt(variance + 1e-06) * (1.0 + modulate[0]) + modulate[1]
    normed_b = normed.astype(jnp.bfloat16)
    columns = jnp.einsum(
        "rnd,dc->rnc",
        lax.all_gather(normed_b, "blk", axis=1, tiled=True),
        qkv_cols,
        preferred_element_type=jnp.float32,
    ).astype(jnp.bfloat16)
    projected = lax.all_to_all(columns, "blk", split_axis=1, concat_axis=2, tiled=True)
    num_req, num_rows, width = layer_in.shape
    queries = projected[:, :, :width]
    new_keys = projected[:, :, width : 2 * width]
    new_values = projected[:, :, 2 * width :]
    use_fresh = (fresh_own == 1)[:, None, None]
    keys = jnp.where(use_fresh, new_keys, old_keys)
    values = jnp.where(use_fresh, new_values, old_values)
    num_heads = width // 64
    num_blocks = live.shape[1]
    q_heads = queries.reshape(num_req, num_rows, num_heads, 64)
    live_float = live.astype(jnp.float32)
    run_max = jnp.full((num_req, num_heads, num_rows), -1e30, jnp.float32)
    key_piece = lax.all_gather(keys, "blk", axis=1, tiled=True)
    value_piece = lax.all_gather(values, "blk", axis=1, tiled=True)
    piece_rows = key_piece.shape[1]
    key_heads = key_piece.reshape(num_req, piece_rows, num_heads, 64)
    value_heads = value_piece.reshape(num_req, piece_rows, num_heads, 64)
    scores = (
        jnp.einsum("qrhd,qnhd->qhrn", q_heads, key_heads, preferred_element_type=jnp.float32)
        * 0.125
    )
    block_ids = jnp.arange(piece_rows) // num_rows
    one_hot = (block_ids[:, None] == jnp.arange(num_blocks)[None, :]).astype(jnp.float32)
    usable = jnp.einsum("qb,nb->qn", live_float, one_hot) > 0.5
    usable = usable[:, None, None, :]
    scores = jnp.where(usable, scores, -1e30)
    new_max = jnp.maximum(run_max, jnp.max(scores, axis=-1))
    weights = jnp.where(usable, jnp.exp(scores - new_max[..., None]), 0.0)
    new_sum = jnp.sum(weights, axis=-1)
    new_acc = jnp.einsum(
        "qhrn,qnhd->qhrd", weights, value_heads.astype(jnp.float32), precision=lax.Precision.HIGHEST
    )
    attn = new_acc / new_sum[..., None]
    attn = jnp.transpose(attn, (0, 2, 1, 3)).reshape(num_req, num_rows, width).astype(jnp.bfloat16)
    out_part = jnp.einsum(
        "rnd,dc->rnc",
        lax.all_gather(attn, "blk", axis=1, tiled=True),
        out_cols,
        preferred_element_type=jnp.float32,
    ).astype(jnp.bfloat16)
    mixed_back = lax.all_to_all(out_part, "blk", split_axis=1, concat_axis=2, tiled=True)
    return (stream + modulate[2] * mixed_back.astype(jnp.float32)).astype(jnp.bfloat16)


def pick_request(array, req_idx):
    return lax.dynamic_index_in_dim(array, req_idx, 0, keepdims=True)


def per_device_by_token(hidden, qkv_weight, out_weight, modulation, timestep, fresh, live, k_stale, v_stale):
    section_idx = lax.axis_index("section")
    block_idx = lax.axis_index("blk")
    steps_all = modulation.shape[1]
    pick_row = (jnp.arange(steps_all) == timestep[0]).astype(jnp.float32)
    modulate = jnp.einsum("t,tcd->cd", pick_row, modulation[0], precision=lax.Precision.HIGHEST)
    num_blocks = fresh.shape[2]
    own_column = (jnp.arange(num_blocks) == block_idx).astype(jnp.int32)
    fresh_own = jnp.sum(fresh[0] * own_column[None, :], axis=1)
    qkv_cols = qkv_weight[0]
    out_cols = out_weight[0]
    old_keys = k_stale[0]
    old_values = v_stale[0]
    num_req = hidden.shape[0]
    received = jnp.zeros_like(hidden[0:1])
    first_out = []
    second_out = []
    for tick_idx in range(num_req + 1):
        if tick_idx < num_req:
            own_input = hidden[tick_idx : tick_idx + 1]
        else:
            own_input = jnp.zeros_like(hidden[0:1])
        layer_in = jnp.where(section_idx == 0, own_input, received)
        req_idx = jnp.clip(tick_idx - section_idx, 0, num_req - 1)
        layer_out = attend(
            layer_in,
            qkv_cols,
            out_cols,
            modulate,
            pick_request(fresh_own, req_idx),
            pick_request(old_keys, req_idx),
            pick_request(old_values, req_idx),
            pick_request(live, req_idx),
        )
        if tick_idx < num_req:
            first_out.append(layer_out)
            received = from_behind(layer_out, "section", 1)
        if tick_idx >= 1:
            second_out.append(layer_out)
    result = jnp.where(
        section_idx == 0, jnp.concatenate(first_out, axis=0), jnp.concatenate(second_out, axis=0)
    )
    return result[None]


HEAD = 64
BF16 = jnp.bfloat16
F32 = jnp.float32
NT = (((1,), (1,)), ((), ()))
VMEM = pl.BlockSpec(memory_space=pltpu.VMEM)
SMEM = pl.BlockSpec(memory_space=pltpu.SMEM)
HBM = pl.BlockSpec(memory_space=pltpu.HBM)
ANY = pl.BlockSpec(memory_space=pl.ANY)


def call(body, outs, scratch, cost, *args, specs=None, spare=40 << 20):
    flops, moved = cost
    return pl.pallas_call(
        body,
        out_shape=outs,
        in_specs=specs or [VMEM] * len(args),
        out_specs=jax.tree.map(lambda _: VMEM, outs),
        scratch_shapes=scratch,
        compiler_params=pltpu.CompilerParams(vmem_limit_bytes=(64 << 20) - spare),
        cost_estimate=pl.CostEstimate(flops=flops, bytes_accessed=moved, transcendentals=0),
    )(*args)


def dot_nt(left, right):
    return lax.dot_general(left, right, NT, preferred_element_type=F32)


def halves(columns):
    mid = columns.shape[0] // 2
    return jnp.concatenate([columns[:mid], columns[mid:]], axis=1)


def pack(cols):
    return jnp.concatenate([cols[:, :128], halves(cols[:, 128:])], axis=0)


def unpack(packed):
    tokens = packed.shape[0] // 3 * 2
    last = packed[tokens:]
    return jnp.concatenate(
        [packed[:tokens], jnp.concatenate([last[:, :HEAD], last[:, HEAD:]], axis=0)], axis=1
    )


def pack_by_parity(cols, odd):
    mid = cols.shape[0] // 2
    even_form = pack(cols)
    odd_form = jnp.concatenate(
        [
            cols[:, HEAD:],
            jnp.concatenate([cols[mid:, :HEAD], cols[:mid, :HEAD]], axis=1),
        ],
        axis=0,
    )
    return jnp.where(odd, odd_form, even_form)


def assemble(blocks, whole, by_heads=False):
    tokens = whole.shape[0]
    n = blocks.shape[0]
    for d in range(0, n, 2):
        even, odd = [group * pow(3, -1, n) % n if by_heads else group for group in (d, d + 1)]
        even_last, odd_last = blocks[even, tokens:].astype(F32), blocks[odd, tokens:].astype(F32)
        left = lax.broadcasted_iota(jnp.int32, even_last.shape, 1) < HEAD
        first = jnp.where(left, even_last, odd_last)
        second = pltpu.roll(jnp.where(left, odd_last, even_last), HEAD, 1)
        at = d // 2 * 384
        whole[:, at : at + 128] = blocks[even, :tokens].astype(whole.dtype)
        whole[:, at + 128 : at + 256] = jnp.concatenate([first, second], axis=0).astype(whole.dtype)
        whole[:, at + 256 : at + 384] = blocks[odd, :tokens].astype(whole.dtype)


def own_columns(ref, rows, me):
    pair = ref[rows, pl.ds(pl.multiple_of(me // 2 * 384, 128), 384)]
    return jnp.where((me & 1) == 1, pair[:, 192:], pair[:, :192])


def norm_into(stream, mod, normed):
    tokens, width = stream.shape
    step = 128
    total = jnp.zeros((tokens, step), F32)
    for at in range(0, width, step):
        total += stream[:, at : at + step]
    center = jnp.sum(total, axis=-1, keepdims=True) / width
    total = jnp.zeros((tokens, step), F32)
    for at in range(0, width, step):
        off = stream[:, at : at + step] - center
        total += off * off
    variance = jnp.sum(total, axis=-1, keepdims=True) / width
    spread = 1.0 / jnp.sqrt(variance + 1e-06)
    for at in range(0, width, step):
        part = (stream[:, at : at + step] - center) * spread
        part = part * (1.0 + mod[0, :, at : at + step]) + mod[1, :, at : at + step]
        normed[:, at : at + step] = part.astype(BF16)


def own_or_other(layer, own, other):
    return jnp.where(lax.axis_index("section") == layer, own, other)


def dot_into(layer, left, own, other, product):
    def into(weight):
        product[...] = dot_nt(left[...], weight[...]).astype(product.dtype)

    held = lax.axis_index("section") == layer
    pl.when(held)(lambda: into(own))
    pl.when(jnp.logical_not(held))(lambda: into(other))


def normalise(layer, stream, mod, other_mod, normed, residual, scales):
    scales[...] = own_or_other(layer, mod[...], other_mod[...])
    norm_into(stream, scales, normed)
    residual[...] = own_columns(stream, slice(None), lax.axis_index("blk")).astype(BF16)


def project(layer, stream, own, other, mod, other_mod, chunks, residual, scales, normed, columns):
    normalise(layer, stream, mod, other_mod, normed, residual, scales)
    dot_into(layer, normed, own, other, columns)
    for j, chunk in enumerate(chunks):
        chunk[...] = pack(columns[:, 192 * j : 192 * j + 192])


def first_projection(arrived, own, other, mod, other_mod, chunk0, chunk1, chunk2, residual, stream, *scratch):
    n = arrived.shape[0]
    rows = stream.shape[0] // n
    for b in range(n):
        stream[rows * b : rows * b + rows, :] = arrived[b, :rows, :].astype(F32)
    project(0, stream, own, other, mod, other_mod, (chunk0, chunk1, chunk2), residual, *scratch)


def next_projection(blocks, own, other, mod, other_mod, chunk0, chunk1, chunk2, residual, stream, *scratch):
    assemble(blocks, stream)
    project(1, stream, own, other, mod, other_mod, (chunk0, chunk1, chunk2), residual, *scratch)


def attention(layer, chunk0, chunk1, chunk2, old, fresh, other_fresh, live, other_out, attn):
    n = attn.shape[0]
    me, request = lax.axis_index("blk"), lax.axis_index("section")
    first = lax.rem(lax.rem(3 * me, n), 3)
    got = [unpack(chunk[...]) for chunk in (chunk0, chunk1, chunk2)]

    def kind(of):
        at = lax.rem(first + of, 3)
        return jnp.where(at == 0, got[0], jnp.where(at == 1, got[1], got[2]))

    queries = kind(0)
    tokens, width = queries.shape
    heads = width // HEAD
    rows = tokens // n
    token = lax.broadcasted_iota(jnp.int32, (tokens, 1), 0)
    is_fresh = jnp.zeros((tokens, 1), jnp.int32)
    for b in range(n):
        flag = own_or_other(layer, fresh[0, request, b], other_fresh[0, request, b])
        is_fresh = jnp.where(token >= b * rows, flag, is_fresh)
    is_fresh = is_fresh == 1
    key = lax.broadcasted_iota(jnp.int32, (1, tokens), 1)
    is_live = jnp.zeros((1, tokens), jnp.int32)
    for b in range(n):
        is_live = jnp.where(key >= b * rows, live[request, b], is_live)
    is_live = is_live == 1
    keys = jnp.where(is_fresh, kind(1).astype(F32), old[layer, :, :width].astype(F32)).astype(BF16)
    values = jnp.where(is_fresh, kind(2).astype(F32), old[layer, :, width:].astype(F32)).astype(BF16)
    head_of = lax.broadcasted_iota(jnp.int32, (tokens, width), 1) // HEAD
    queries = queries.astype(F32)
    stacked = jnp.concatenate([jnp.where(head_of == h, queries, 0.0) for h in range(heads)], axis=0)
    scores = dot_nt(stacked.astype(BF16), keys) * 0.125
    scores = jnp.where(is_live, scores, -1e30)
    top = jnp.max(scores, axis=-1, keepdims=True)
    weights = jnp.where(is_live, jnp.exp(scores - top), 0.0)
    total = jnp.sum(weights, axis=-1, keepdims=True)
    mixed = jnp.dot(weights.astype(BF16), values, preferred_element_type=F32) / total
    result = jnp.zeros((tokens, width), F32)
    for h in range(heads):
        result = jnp.where(head_of == h, mixed[h * tokens : (h + 1) * tokens], result)
    packed = pack_by_parity(result, (me & 1) == 1).astype(BF16)
    for d in range(n):
        attn[d] = packed


def layer_columns(layer, blocks, own, other, mod, other_mod, residual, whole, mixed):
    me = lax.axis_index("blk")
    assemble(blocks, whole, by_heads=True)
    dot_into(layer, whole, own, other, mixed)
    gates = own_or_other(layer, mod[2], other_mod[2])
    pairs = [gates[:, at : at + 384] for at in range(0, gates.shape[1], 384)]
    pair = pairs[0]
    for i, other_pair in enumerate(pairs):
        pair = jnp.where(me // 2 == i, other_pair, pair)
    gate = jnp.where((me & 1) == 1, pair[:, 192:], pair[:, :192])
    return (residual[...].astype(F32) + gate * mixed[...].astype(F32)).astype(BF16).astype(F32)


def first_output(blocks, own, other, mod, other_mod, residual, copies, kept, *scratch):
    columns = layer_columns(0, blocks, own, other, mod, other_mod, residual, *scratch)
    packed = pack_by_parity(columns, (lax.axis_index("blk") & 1) == 1).astype(BF16)
    for d in range(copies.shape[0]):
        copies[d] = packed
    kept[...] = columns


def last_output(blocks, own, other, mod, other_mod, residual, kept, by_token, columns, *scratch):
    columns[...] = layer_columns(1, blocks, own, other, mod, other_mod, residual, *scratch)
    n = by_token.shape[0] // 2
    rows = columns.shape[0] // n
    for layer, outs in enumerate((kept, columns)):
        for b in range(n):
            by_token[layer * n + b, :rows, :] = outs[rows * b : rows * b + rows, :].astype(BF16)


def first_exchange(hidden, old_keys, old_values, other_keys, other_values, leaving, held, sems):
    copies = [
        pltpu.make_async_copy(ref, held.at[i], sems.at[i])
        for i, ref in enumerate((hidden, old_keys, old_values, other_keys, other_values))
    ]
    for copy in copies:
        copy.start()
    rows, reqs, width = hidden.shape
    n = leaving.shape[0]
    columns = width // n
    first = lax.axis_index("section") == 0
    for copy in copies:
        copy.wait()

    def of_request(which):
        own = [held[which, i].astype(F32) for i in range(rows)]
        return jnp.concatenate([jnp.where(first, pair[:1], pair[1:]) for pair in own], axis=0)

    mine, *arrays = [of_request(which) for which in range(5)]
    mine = mine.astype(BF16)
    own, other = arrays[:2], arrays[2:]
    stale = [jnp.where(first, a, b) for a, b in zip(own, other)] + [jnp.where(first, b, a) for a, b in zip(own, other)]
    for b in range(n):
        at = columns * (3 * b % n)
        block = jnp.concatenate([array[:, at : at + columns] for array in stale], axis=1)
        leaving[b, :rows, :] = mine
        for i in range(rows):
            leaving[b, rows : rows + 1, i * 4 * columns : (i + 1) * 4 * columns] = block[i : i + 1].astype(BF16)


def stale_by_token(arrived, old, rows):
    n = arrived.shape[0]
    per = rows.shape[1] // n
    wide = rows.shape[2]
    for b in range(n):
        flat = arrived[b, per : per + 1, :].astype(F32)
        for i in range(per):
            for layer in range(2):
                at = (i * 2 + layer) * wide
                rows[layer, per * b + i : per * b + i + 1, :] = flat[:, at : at + wide]
    old[...] = rows[...].astype(BF16)


def to_rows(arrived, out, rows):
    n = arrived.shape[0] // 2
    per, columns = out.shape[0], arrived.shape[2]
    for s in range(2):
        for b in range(n):
            rows[s, :per, columns * b : columns * b + columns] = arrived[s * n + b, :per, :].astype(F32)
    for i in range(per):
        out[i] = jnp.concatenate([rows[s, i : i + 1, :] for s in range(2)], axis=0).astype(BF16)


def exchange(blocks, axis):
    return lax.all_to_all(blocks, axis, split_axis=0, concat_axis=0, tiled=True)


def swap_sections(array):
    return lax.ppermute(array, "section", [(0, 1), (1, 0)])


def by_heads(chunks, n):
    inverse = pow(3, -1, n)
    return [
        lax.ppermute(chunk, "blk", [(b, (b + inverse * j) % n) for b in range(n)]) if j else chunk
        for j, chunk in enumerate(chunks)
    ]


def per_device(hidden, qkv_weight, out_weight, modulation, timestep, fresh, live, k_stale, v_stale):
    n = lax.axis_size("blk")
    columns = out_weight.shape[2]
    reqs, rows, width = hidden.shape
    if not (
        columns == 3 * HEAD
        and n % 3 == 1
        and n & (n - 1) == 0
        and reqs == lax.axis_size("section") == 2
        and rows <= 4
    ):
        return per_device_by_token(
            hidden, qkv_weight, out_weight, modulation, timestep, fresh, live, k_stale, v_stale
        )
    tokens = n * rows
    shape = jax.ShapeDtypeStruct
    packed = shape((tokens * 3 // 2, 128), BF16)
    copies = shape((n, tokens * 3 // 2, 128), BF16)
    cols = shape((tokens, columns), BF16)
    own_qkv = jnp.swapaxes(qkv_weight[0], 0, 1)
    own_out = jnp.swapaxes(out_weight[0], 0, 1)
    steps = jnp.transpose(modulation, (1, 2, 0, 3))
    mod = lax.dynamic_index_in_dim(steps, timestep[0], 0, keepdims=False)
    old_keys = jnp.transpose(k_stale[0], (1, 0, 2))
    old_values = jnp.transpose(v_stale[0], (1, 0, 2))

    leaving = call(
        first_exchange,
        shape((n, 4, width), BF16),
        [pltpu.VMEM((5, rows, reqs, width), BF16), pltpu.SemaphoreType.DMA((5,))],
        (0, 1000000),
        jnp.transpose(hidden, (1, 0, 2)),
        old_keys,
        old_values,
        swap_sections(old_keys),
        swap_sections(old_values),
        specs=[HBM] * 3 + [ANY] * 2,
        spare=4 << 20,
    )
    leaving, other_mod, own_qkv = lax.optimization_barrier((leaving, swap_sections(mod), own_qkv))
    mods = (mod, other_mod)
    qkv = (lax.ppermute(own_qkv, "section", [(0, 0), (1, 1)]), swap_sections(own_qkv))
    arrived, own_out, own_fresh = lax.optimization_barrier((exchange(leaving, "blk"), own_out, fresh))
    out = (own_out, swap_sections(own_out))
    flags = (fresh, swap_sections(own_fresh))

    blocks = arrived
    for layer in range(2):
        *chunks, residual = call(
            next_projection if layer else first_projection,
            [packed, packed, packed, cols],
            [
                pltpu.VMEM((tokens, width), F32),
                pltpu.VMEM(mod.shape, F32),
                pltpu.VMEM((tokens, width), BF16),
                pltpu.VMEM((tokens, 3 * columns), BF16),
            ],
            (2 * tokens * width * 3 * columns, 8 * width * columns),
            blocks,
            *qkv,
            *mods,
        )
        if layer == 0:
            arrived, chunks[1] = lax.optimization_barrier((arrived, chunks[1]))
            old = call(
                stale_by_token,
                shape((2, tokens, 2 * columns), BF16),
                [pltpu.VMEM((2, tokens, 2 * columns), F32)],
                (0, 200000),
                arrived,
            )
        attn = call(
            functools.partial(attention, layer),
            copies,
            [],
            (8 * tokens * tokens * columns, 300000),
            *by_heads(chunks, n),
            old,
            *flags,
            live,
            out[1],
            specs=[VMEM] * 4 + [SMEM] * 3 + [ANY],
        )
        args = (exchange(attn, "blk"), *out, *mods, residual)
        cost = (2 * tokens * width * columns, 4 * width * columns)
        held = [pltpu.VMEM((tokens, width), BF16), pltpu.VMEM((tokens, columns), BF16)]
        if layer == 0:
            leaving, kept = call(first_output, [copies, shape((tokens, columns), F32)], held, cost, *args)
            blocks = exchange(leaving, "blk")
        else:
            leaving = call(
                last_output,
                shape((2 * n, 4, columns), BF16),
                [pltpu.VMEM((tokens, columns), F32)] + held,
                cost,
                *args,
                kept,
            )
    result = call(
        to_rows,
        shape((rows, reqs, width), BF16),
        [pltpu.VMEM((2, 8, width), F32)],
        (0, 100000),
        exchange(leaving, ("section", "blk")),
    )
    return jnp.transpose(result, (1, 0, 2))[None]


def solution(mesh):
    return jax.shard_map(
        per_device,
        mesh=mesh,
        in_specs=(
            P(None, "blk", None),
            P("section", None, "blk"),
            P("section", None, "blk"),
            P("section", None, None, None),
            P(),
            P("section", None, None),
            P(),
            P("section", None, "blk", None),
            P("section", None, "blk", None),
        ),
        out_specs=P("section", None, "blk", None),
        check_vma=False,
    )
```

profile of v0, /device:TPU:0, one launch (start us, length us, event | category | flops | bytes accessed | tf_op | source)
XLA Modules:
  0.0 100.1 jit_solution(3639922465868432861)
XLA Ops:
  0.0 0.0 copy-start
  0.0 0.5 collective-permute-start
  0.5 0.1 collective-permute-start.1
  1.2 0.3 copy-done
  1.5 0.5 collective-permute-start.2
  2.0 0.0 collective-permute-done.other_keys
  2.0 0.0 copy-start.4
  2.0 0.0 collective-permute-done.1.other_values
  2.0 0.0 copy-start.5
  2.0 0.6 copy-done.4
  2.6 0.0 copy-done.5
  2.6 1.9 %shard_map.91 = bf16[16,4,3072]{2,1,0:T(4,128)(2,1)} custom-call(bf16[3,2,3072]{2,1,0:T(2,128)(2,1)} %bitcast.25, bf16[3,2,3072]{2,1,0:T(2,128)(2,1)} %bitcast.27, bf16[3,2,3072]{2,1,0:T(2,128)(2,1)} %bitcast.29, bf16[3,2,3072]{2,1,0:T(2,128)(2,1)} %copy-done.4, bf16[3,2,3072]{2,1,0:T(2,128)(2,1)} %copy-done.5), custom_call_target="tpu_custom_call" | custom-call | bytes 1000000 | tf_op jit(solution)/shard_map/pallas_call | solution.py:135
  4.5 0.0 collective-permute-done.2.other_mod
  4.5 0.1 collective-permute-start.4
  4.6 2.0 %collective-permute-start.3 = (bf16[576,3072]{1,0:T(8,128)(2,1)}, bf16[576,3072]{1,0:T(8,128)(2,1)S(1)}, u32[]{:S(2)}, u32[]{:S(2)}) collective-permute-start(bf16[576,3072]{1,0:T(8,128)(2,1)} %bitcast.31), channel_id=1, source_target_pairs={{0,0},{16,16},{1,1},{17,17},{2,2},{18,18},{3,3},{19,19},{4,4},{20,... | collective-permute-start | bytes 10616840 | tf_op jit(solution)/shard_map/ppermute | solution.py:442
  6.6 21.1 %all_to_all.25.arrived = bf16[16,4,3072]{2,1,0:T(4,128)(2,1)S(1)} all-to-all(bf16[16,4,3072]{2,1,0:T(4,128)(2,1)} %shard_map.91), channel_id=1, replica_groups=mesh['section'=2,'blk'=16] {'blk'}, dimensions={0} | all-to-all | bytes 786432 | tf_op jit(solution)/shard_map/all_to_all | solution.py:386
  27.7 0.0 copy-start.2
  27.7 0.0 copy-start.3
  27.7 0.0 collective-permute-start.8
  27.7 0.0 collective-permute-done.4.other
  27.7 0.0 collective-permute-done.3.own
  27.7 1.7 %shard_map.92 = (bf16[72,128]{1,0:T(8,128)(2,1)S(1)}, bf16[72,128]{1,0:T(8,128)(2,1)S(1)}, bf16[72,128]{1,0:T(8,128)(2,1)S(1)}, bf16[48,192]{1,0:T(8,128)(2,1)S(1)}) custom-call(bf16[16,4,3072]{2,1,0:T(4,128)(2,1)S(1)} %all_to_all.25.arrived, bf16[576,3072]{1,0:T(8,128)(2,1)S(1)} %collective-permute-done.3.own, ...), custom_call_target="tpu_custom_call" | custom-call | flops 169869312 | bytes 4718592 | tf_op jit(solution)/shard_map/pallas_call | solution.py:135
  29.5 0.0 copy-start.1
  29.5 0.8 collective-permute-start.5
  30.3 2.1 %collective-permute-start.6 = (bf16[72,128]{1,0:T(8,128)(2,1)S(1)}, bf16[72,128]{1,0:T(8,128)(2,1)S(1)}, u32[]{:S(2)}, u32[]{:S(2)}) collective-permute-start(bf16[72,128]{1,0:T(8,128)(2,1)S(1)} %get-tuple-element.30), channel_id=1, source_target_pairs={{0,6},{1,7},{2,8},{3,9},{4,10},{5,11},{6,12},{7,13},{8,14},{9,15},... | collective-permute-start | bytes 55304 | tf_op jit(solution)/shard_map/ppermute | solution.py:396
  32.4 0.0 copy-done.2
  32.4 0.0 collective-permute-start.7
  32.4 0.1 shard_map.93.old
  32.6 1.0 %collective-permute-done.7.other_fresh = s32[1,2,16]{2,1,0:T(2,128)S(1)} collective-permute-done((s32[1,2,16]{2,1,0:T(2,128)S(1)}, s32[1,2,16]{2,1,0:T(2,128)S(1)}, u32[]{:S(2)}, u32[]{:S(2)}) %collective-permute-start.7) | collective-permute-done | bytes 160 | tf_op jit(solution)/shard_map/ppermute | solution.py:390
  33.6 0.0 collective-permute-done.8.other_out.other
  33.6 0.6 collective-permute-done.5.chunk1
  34.2 1.7 %collective-permute-done.6.chunk2 = bf16[72,128]{1,0:T(8,128)(2,1)S(1)} collective-permute-done((bf16[72,128]{1,0:T(8,128)(2,1)S(1)}, bf16[72,128]{1,0:T(8,128)(2,1)S(1)}, u32[]{:S(2)}, u32[]{:S(2)}) %collective-permute-start.6) | collective-permute-done | bytes 18464 | tf_op jit(solution)/shard_map/ppermute | solution.py:396
  35.9 0.0 copy-done.3
  35.9 1.3 %shard_map.94 = bf16[16,72,128]{2,1,0:T(8,128)(2,1)S(1)} custom-call(bf16[72,128]{1,0:T(8,128)(2,1)S(1)} %get-tuple-element.27.chunk0, bf16[72,128]{1,0:T(8,128)(2,1)S(1)} %collective-permute-done.5.chunk1, bf16[72,128]{1,0:T(8,128)(2,1)S(1)} %collective-permute-done.6.chunk2, bf16[2,48,384]{2,1,0:T(8,128)(2,1)S(1)} %shard_map.93.old, ...), custom_call_target="tpu_custom_call" | custom-call | flops 3538944 | bytes 300000 | tf_op jit(solution)/shard_map/pallas_call | solution.py:135
  37.2 14.9 %all_to_all.26.blocks = bf16[16,72,128]{2,1,0:T(8,128)(2,1)S(1)} all-to-all(bf16[16,72,128]{2,1,0:T(8,128)(2,1)S(1)} %shard_map.94), channel_id=1, replica_groups=mesh['section'=2,'blk'=16] {'blk'}, dimensions={0} | all-to-all | bytes 589824 | tf_op jit(solution)/shard_map/all_to_all | solution.py:386
  52.0 0.0 copy-done.1
  52.1 0.9 shard_map.95
  52.9 13.1 %all_to_all.27.blocks = bf16[16,72,128]{2,1,0:T(8,128)(2,1)S(1)} all-to-all(bf16[16,72,128]{2,1,0:T(8,128)(2,1)S(1)} %get-tuple-element.35), channel_id=1, replica_groups=mesh['section'=2,'blk'=16] {'blk'}, dimensions={0} | all-to-all | bytes 589824 | tf_op jit(solution)/shard_map/all_to_all | solution.py:386
  66.1 1.7 %shard_map.96 = (bf16[72,128]{1,0:T(8,128)(2,1)S(1)}, bf16[72,128]{1,0:T(8,128)(2,1)S(1)}, bf16[72,128]{1,0:T(8,128)(2,1)S(1)}, bf16[48,192]{1,0:T(8,128)(2,1)S(1)}) custom-call(bf16[16,72,128]{2,1,0:T(8,128)(2,1)S(1)} %all_to_all.27.blocks, bf16[576,3072]{1,0:T(8,128)(2,1)S(1)} %collective-permute-done.3.own, ...), custom_call_target="tpu_custom_call" | custom-call | flops 169869312 | bytes 4718592 | tf_op jit(solution)/shard_map/pallas_call | solution.py:135
  67.8 0.9 collective-permute-start.9
  68.6 2.1 %collective-permute-start.10 = (bf16[72,128]{1,0:T(8,128)(2,1)S(1)}, bf16[72,128]{1,0:T(8,128)(2,1)S(1)}, u32[]{:S(2)}, u32[]{:S(2)}) collective-permute-start(bf16[72,128]{1,0:T(8,128)(2,1)S(1)} %get-tuple-element.38), channel_id=1, source_target_pairs={{0,6},{1,7},{2,8},{3,9},{4,10},{5,11},{6,12},{7,13},{8,14},{9,15},... | collective-permute-start | bytes 55304 | tf_op jit(solution)/shard_map/ppermute | solution.py:396
  70.7 1.7 %collective-permute-done.9.chunk1 = bf16[72,128]{1,0:T(8,128)(2,1)S(1)} collective-permute-done((bf16[72,128]{1,0:T(8,128)(2,1)S(1)}, bf16[72,128]{1,0:T(8,128)(2,1)S(1)}, u32[]{:S(2)}, u32[]{:S(2)}) %collective-permute-start.9) | collective-permute-done | bytes 18464 | tf_op jit(solution)/shard_map/ppermute | solution.py:396
  72.4 1.8 %collective-permute-done.10.chunk2 = bf16[72,128]{1,0:T(8,128)(2,1)S(1)} collective-permute-done((bf16[72,128]{1,0:T(8,128)(2,1)S(1)}, bf16[72,128]{1,0:T(8,128)(2,1)S(1)}, u32[]{:S(2)}, u32[]{:S(2)}) %collective-permute-start.10) | collective-permute-done | bytes 18464 | tf_op jit(solution)/shard_map/ppermute | solution.py:396
  74.2 1.3 %shard_map.97 = bf16[16,72,128]{2,1,0:T(8,128)(2,1)S(1)} custom-call(bf16[72,128]{1,0:T(8,128)(2,1)S(1)} %get-tuple-element.36.chunk0, bf16[72,128]{1,0:T(8,128)(2,1)S(1)} %collective-permute-done.9.chunk1, bf16[72,128]{1,0:T(8,128)(2,1)S(1)} %collective-permute-done.10.chunk2, bf16[2,48,384]{2,1,0:T(8,128)(2,1)S(1)} %shard_map.93.old, ...), custom_call_target="tpu_custom_call" | custom-call | flops 3538944 | bytes 300000 | tf_op jit(solution)/shard_map/pallas_call | solution.py:135
  75.5 13.5 %all_to_all.28.blocks = bf16[16,72,128]{2,1,0:T(8,128)(2,1)S(1)} all-to-all(bf16[16,72,128]{2,1,0:T(8,128)(2,1)S(1)} %shard_map.97), channel_id=1, replica_groups=mesh['section'=2,'blk'=16] {'blk'}, dimensions={0} | all-to-all | bytes 589824 | tf_op jit(solution)/shard_map/all_to_all | solution.py:386
  88.9 0.7 shard_map.98
  89.6 9.7 %all_to_all.29.arrived = bf16[32,4,192]{2,1,0:T(4,128)(2,1)S(1)} all-to-all(bf16[32,4,192]{2,1,0:T(4,128)(2,1)S(1)} %shard_map.98), channel_id=1, replica_groups=mesh['section'=2,'blk'=16] {'section','blk'}, dimensions={0} | all-to-all | bytes 98304 | tf_op jit(solution)/shard_map/all_to_all | solution.py:386
  99.4 0.8 shard_map.99
  (1 shorter events, 0.0 us)
Async XLA Ops:
  0.0 1.5 %copy-start = (f32[1,50,3,3072]{3,0,2,1:T(1,128)S(1)}, f32[1,50,3,3072]{3,0,2,1:T(1,128)}, u32[]{:S(2)}) copy-start(f32[1,50,3,3072]{3,0,2,1:T(1,128)} %param.12) | copy-start | bytes 5529604
  0.0 2.0 %collective-permute-start = (bf16[3,2,3072]{2,1,0:T(2,128)(2,1)}, bf16[3,2,3072]{2,1,0:T(2,128)(2,1)S(1)}, u32[]{:S(2)}, u32[]{:S(2)}) collective-permute-start(bf16[3,2,3072]{2,1,0:T(2,128)(2,1)} %bitcast.26), channel_id=1, source_target_pairs={{0,16},{16,0},{1,17},{17,1},{2,18},{18,2},{3,19},{19,3},{4,20},{20... | collective-permute-start | bytes 110600 | tf_op jit(solution)/shard_map/ppermute | solution.py:390
  0.5 1.5 %collective-permute-start.1 = (bf16[3,2,3072]{2,1,0:T(2,128)(2,1)}, bf16[3,2,3072]{2,1,0:T(2,128)(2,1)S(1)}, u32[]{:S(2)}, u32[]{:S(2)}) collective-permute-start(bf16[3,2,3072]{2,1,0:T(2,128)(2,1)} %bitcast.28), channel_id=1, source_target_pairs={{0,16},{16,0},{1,17},{17,1},{2,18},{18,2},{3,19},{19,3},{4,20},{20... | collective-permute-start | bytes 110600 | tf_op jit(solution)/shard_map/ppermute | solution.py:390
  1.5 3.0 %collective-permute-start.2 = (f32[3,1,3072]{2,1,0:T(1,128)S(1)}, f32[3,1,3072]{2,1,0:T(1,128)S(1)}, u32[]{:S(2)}, u32[]{:S(2)}) collective-permute-start(f32[3,1,3072]{2,1,0:T(1,128)S(1)} %dynamic-slice_bitcast_fusion.mod), channel_id=1, source_target_pairs={{0,16},{16,0},{1,17},{17,1},{2,18},{18,2},{3,19},{19,3},{4,20},{20... | collective-permute-start | bytes 110600 | tf_op jit(solution)/shard_map/ppermute | solution.py:390
  2.0 0.6 copy-start.4
  2.0 0.6 copy-start.5
  4.5 23.3 %collective-permute-start.4 = (bf16[576,3072]{1,0:T(8,128)(2,1)}, bf16[576,3072]{1,0:T(8,128)(2,1)S(1)}, u32[]{:S(2)}, u32[]{:S(2)}) collective-permute-start(bf16[576,3072]{1,0:T(8,128)(2,1)} %bitcast.30), channel_id=1, source_target_pairs={{0,16},{16,0},{1,17},{17,1},{2,18},{18,2},{3,19},{19,3},{4,20},{20... | collective-permute-start | bytes 10616840 | tf_op jit(solution)/shard_map/ppermute | solution.py:390
  4.6 23.1 %collective-permute-start.3 = (bf16[576,3072]{1,0:T(8,128)(2,1)}, bf16[576,3072]{1,0:T(8,128)(2,1)S(1)}, u32[]{:S(2)}, u32[]{:S(2)}) collective-permute-start(bf16[576,3072]{1,0:T(8,128)(2,1)} %bitcast.31), channel_id=1, source_target_pairs={{0,0},{16,16},{1,1},{17,17},{2,2},{18,18},{3,3},{19,19},{4,4},{20,... | collective-permute-start | bytes 10616840 | tf_op jit(solution)/shard_map/ppermute | solution.py:442
  27.7 4.7 %copy-start.2 = (s32[1,2,16]{2,1,0:T(2,128)S(1)}, s32[1,2,16]{2,1,0:T(2,128)}, u32[]{:S(2)}) copy-start(s32[1,2,16]{2,1,0:T(2,128)} %fresh.3) | copy-start | bytes 388
  27.7 8.2 %copy-start.3 = (s32[2,16]{1,0:T(2,128)S(1)}, s32[2,16]{1,0:T(2,128)}, u32[]{:S(2)}) copy-start(s32[2,16]{1,0:T(2,128)} %live.3) | copy-start | bytes 388
  27.7 5.8 %collective-permute-start.8 = (bf16[192,3072]{1,0:T(8,128)(2,1)}, bf16[192,3072]{1,0:T(8,128)(2,1)S(1)}, u32[]{:S(2)}, u32[]{:S(2)}) collective-permute-start(bf16[192,3072]{1,0:T(8,128)(2,1)} %bitcast.22), channel_id=1, source_target_pairs={{0,16},{16,0},{1,17},{17,1},{2,18},{18,2},{3,19},{19,3},{4,20},{20... | collective-permute-start | bytes 3538952 | tf_op jit(solution)/shard_map/ppermute | solution.py:390
  29.5 22.6 %copy-start.1 = (bf16[1,3072,192]{1,2,0:T(8,128)(2,1)S(1)}, bf16[1,3072,192]{1,2,0:T(8,128)(2,1)}, u32[]{:S(2)}) copy-start(bf16[1,3072,192]{1,2,0:T(8,128)(2,1)} %param.11) | copy-start | bytes 3538948
  29.5 4.7 %collective-permute-start.5 = (bf16[72,128]{1,0:T(8,128)(2,1)S(1)}, bf16[72,128]{1,0:T(8,128)(2,1)S(1)}, u32[]{:S(2)}, u32[]{:S(2)}) collective-permute-start(bf16[72,128]{1,0:T(8,128)(2,1)S(1)} %get-tuple-element.29), channel_id=1, source_target_pairs={{0,11},{1,12},{2,13},{3,14},{4,15},{5,0},{6,1},{7,2},{8,3},{9,4},{... | collective-permute-start | bytes 55304 | tf_op jit(solution)/shard_map/ppermute | solution.py:396
  30.3 5.6 %collective-permute-start.6 = (bf16[72,128]{1,0:T(8,128)(2,1)S(1)}, bf16[72,128]{1,0:T(8,128)(2,1)S(1)}, u32[]{:S(2)}, u32[]{:S(2)}) collective-permute-start(bf16[72,128]{1,0:T(8,128)(2,1)S(1)} %get-tuple-element.30), channel_id=1, source_target_pairs={{0,6},{1,7},{2,8},{3,9},{4,10},{5,11},{6,12},{7,13},{8,14},{9,15},... | collective-permute-start | bytes 55304 | tf_op jit(solution)/shard_map/ppermute | solution.py:396
  32.4 1.1 %collective-permute-start.7 = (s32[1,2,16]{2,1,0:T(2,128)S(1)}, s32[1,2,16]{2,1,0:T(2,128)S(1)}, u32[]{:S(2)}, u32[]{:S(2)}) collective-permute-start(s32[1,2,16]{2,1,0:T(2,128)S(1)} %copy-done.2), channel_id=1, source_target_pairs={{0,16},{16,0},{1,17},{17,1},{2,18},{18,2},{3,19},{19,3},{4,20},{20... | collective-permute-start | bytes 392 | tf_op jit(solution)/shard_map/ppermute | solution.py:390
  67.8 4.7 %collective-permute-start.9 = (bf16[72,128]{1,0:T(8,128)(2,1)S(1)}, bf16[72,128]{1,0:T(8,128)(2,1)S(1)}, u32[]{:S(2)}, u32[]{:S(2)}) collective-permute-start(bf16[72,128]{1,0:T(8,128)(2,1)S(1)} %get-tuple-element.37), channel_id=1, source_target_pairs={{0,11},{1,12},{2,13},{3,14},{4,15},{5,0},{6,1},{7,2},{8,3},{9,4},{... | collective-permute-start | bytes 55304 | tf_op jit(solution)/shard_map/ppermute | solution.py:396
  68.6 5.6 %collective-permute-start.10 = (bf16[72,128]{1,0:T(8,128)(2,1)S(1)}, bf16[72,128]{1,0:T(8,128)(2,1)S(1)}, u32[]{:S(2)}, u32[]{:S(2)}) collective-permute-start(bf16[72,128]{1,0:T(8,128)(2,1)S(1)} %get-tuple-element.38), channel_id=1, source_target_pairs={{0,6},{1,7},{2,8},{3,9},{4,10},{5,11},{6,12},{7,13},{8,14},{9,15},... | collective-permute-start | bytes 55304 | tf_op jit(solution)/shard_map/ppermute | solution.py:396
where the time goes:
time: 101 us; the launch traced here: 100 us
  blocking collectives  72.3 us (72%)
  Pallas kernels  10.3 us (10%)
  starting transfers between devices  8.98 us (9%)
  waiting for transfers between devices  6.85 us (7%)
    all_to_all x5, blocking collectives, exchange(): return lax.all_to_all(blocks, axis, split_axis=0, concat_axis=0, tiled=True)  72.3 us
    pallas_call x9, Pallas kernels, call(): pl.pallas_call(body, out_shape=outs, in_specs=specs or [VMEM] * len(args)...  10.3 us
    ppermute x4, starting transfers between devices, by_heads(): lax.ppermute(chunk, 'blk', [(b, (b + inverse * j) % n) for b in range(n)])  5.88 us
    ppermute x4, waiting for transfers between devices, by_heads(): lax.ppermute(chunk, 'blk', [(b, (b + inverse * j) % n) for b in range(n)])  5.81 us
  transfers between devices with their start and end apart: 11, of which 5 were waited for; matrix products, arithmetic and copies ran while one was open for 0% of the time, Pallas kernels for 4%

commit v1 on v0

--- a/solution.py
+++ b/solution.py
@@ -235,35 +235,37 @@
     residual[...] = own_columns(stream, slice(None), lax.axis_index("blk")).astype(BF16)
 
 
-def project(layer, stream, own, other, mod, other_mod, chunks, residual, scales, normed, columns):
-    normalise(layer, stream, mod, other_mod, normed, residual, scales)
-    dot_into(layer, normed, own, other, columns)
+def chunks_of(columns, chunks):
     for j, chunk in enumerate(chunks):
         chunk[...] = pack(columns[:, 192 * j : 192 * j + 192])
 
 
-def first_projection(arrived, own, other, mod, other_mod, chunk0, chunk1, chunk2, residual, stream, *scratch):
+def first_projection(arrived, own, other, mod, other_mod, other_out, chunk0, chunk1, chunk2, residual, stream, scales, normed, columns):
     n = arrived.shape[0]
     rows = stream.shape[0] // n
     for b in range(n):
         stream[rows * b : rows * b + rows, :] = arrived[b, :rows, :].astype(F32)
-    project(0, stream, own, other, mod, other_mod, (chunk0, chunk1, chunk2), residual, *scratch)
-
-
-def next_projection(blocks, own, other, mod, other_mod, chunk0, chunk1, chunk2, residual, stream, *scratch):
+    normalise(0, stream, mod, other_mod, normed, residual, scales)
+    dot_into(0, normed, own, other, columns)
+    chunks_of(columns, (chunk0, chunk1, chunk2))
+
+
+def next_projection(blocks, own, other, mod, other_mod, chunk0, chunk1, chunk2, residual, stream, scales, normed, columns):
     assemble(blocks, stream)
-    project(1, stream, own, other, mod, other_mod, (chunk0, chunk1, chunk2), residual, *scratch)
-
-
-def attention(layer, chunk0, chunk1, chunk2, old, fresh, other_fresh, live, other_out, attn):
+    normalise(1, stream, mod, other_mod, normed, residual, scales)
+    dot_into(1, normed, own, other, columns)
+    chunks_of(columns, (chunk0, chunk1, chunk2))
+
+
+def attention(layer, chunk0, chunk1, chunk2, old, fresh, other_fresh, live, attn):
     n = attn.shape[0]
     me, request = lax.axis_index("blk"), lax.axis_index("section")
     first = lax.rem(lax.rem(3 * me, n), 3)
-    got = [unpack(chunk[...]) for chunk in (chunk0, chunk1, chunk2)]
+    got = [chunk[...].astype(F32) for chunk in (chunk0, chunk1, chunk2)]
 
     def kind(of):
         at = lax.rem(first + of, 3)
-        return jnp.where(at == 0, got[0], jnp.where(at == 1, got[1], got[2]))
+        return unpack(jnp.where(at == 0, got[0], jnp.where(at == 1, got[1], got[2])))
 
     queries = kind(0)
     tokens, width = queries.shape
@@ -280,17 +282,16 @@
     for b in range(n):
         is_live = jnp.where(key >= b * rows, live[request, b], is_live)
     is_live = is_live == 1
-    keys = jnp.where(is_fresh, kind(1).astype(F32), old[layer, :, :width].astype(F32)).astype(BF16)
-    values = jnp.where(is_fresh, kind(2).astype(F32), old[layer, :, width:].astype(F32)).astype(BF16)
+    keys = jnp.where(is_fresh, kind(1), old[layer, :, :width].astype(F32)).astype(BF16)
+    values = jnp.where(is_fresh, kind(2), old[layer, :, width:].astype(F32)).astype(BF16)
     head_of = lax.broadcasted_iota(jnp.int32, (tokens, width), 1) // HEAD
-    queries = queries.astype(F32)
     stacked = jnp.concatenate([jnp.where(head_of == h, queries, 0.0) for h in range(heads)], axis=0)
     scores = dot_nt(stacked.astype(BF16), keys) * 0.125
     scores = jnp.where(is_live, scores, -1e30)
     top = jnp.max(scores, axis=-1, keepdims=True)
     weights = jnp.where(is_live, jnp.exp(scores - top), 0.0)
     total = jnp.sum(weights, axis=-1, keepdims=True)
-    mixed = jnp.dot(weights.astype(BF16), values, preferred_element_type=F32) / total
+    mixed = jnp.dot(weights.astype(BF16), values, preferred_element_type=F32) * (1.0 / total)
     result = jnp.zeros((tokens, width), F32)
     for h in range(heads):
         result = jnp.where(head_of == h, mixed[h * tokens : (h + 1) * tokens], result)
@@ -437,12 +438,15 @@
         specs=[HBM] * 3 + [ANY] * 2,
         spare=4 << 20,
     )
-    leaving, other_mod, own_qkv = lax.optimization_barrier((leaving, swap_sections(mod), own_qkv))
+    leaving, other_mod, other_fresh, sent_qkv, sent_out = lax.optimization_barrier(
+        (leaving, swap_sections(mod), swap_sections(fresh), own_qkv, own_out)
+    )
     mods = (mod, other_mod)
-    qkv = (lax.ppermute(own_qkv, "section", [(0, 0), (1, 1)]), swap_sections(own_qkv))
-    arrived, own_out, own_fresh = lax.optimization_barrier((exchange(leaving, "blk"), own_out, fresh))
-    out = (own_out, swap_sections(own_out))
-    flags = (fresh, swap_sections(own_fresh))
+    flags = (fresh, other_fresh)
+    other_qkv, other_out = swap_sections(sent_qkv), swap_sections(sent_out)
+    out = (own_out, other_out)
+    held_qkv = lax.ppermute(sent_qkv, "section", [(0, 0)])
+    arrived = exchange(leaving, "blk")
 
     blocks = arrived
     for layer in range(2):
@@ -457,8 +461,8 @@
             ],
             (2 * tokens * width * 3 * columns, 8 * width * columns),
             blocks,
-            *qkv,
-            *mods,
+            *((own_qkv, other_qkv, *mods) if layer else (held_qkv, other_qkv, *mods, other_out)),
+            **({} if layer else {"specs": [VMEM] * 5 + [ANY]}),
         )
         if layer == 0:
             arrived, chunks[1] = lax.optimization_barrier((arrived, chunks[1]))
@@ -478,8 +482,7 @@
             old,
             *flags,
             live,
-            out[1],
-            specs=[VMEM] * 4 + [SMEM] * 3 + [ANY],
+            specs=[VMEM] * 4 + [SMEM] * 3,
         )
         args = (exchange(attn, "blk"), *out, *mods, residual)
         cost = (2 * tokens * width * columns, 4 * width * columns)

time: 101 us -> 100 us (0.990)
  blocking collectives: 72.3 us -> 70 us
  starting transfers between devices: 8.98 us -> 11 us
    all_to_all x5, blocking collectives: 72.3 us -> 70 us  [exchange(): return lax.all_to_all(blocks, axis, split_axis=0, concat_axis=0, tiled=True)]
    ppermute x6, waiting for transfers between devices: 1.03 us -> 0.02 us  [swap_sections(): return lax.ppermute(array, 'section', [(0, 1), (1, 0)])]
  transfers between devices with their start and end apart: 11 -> 11, of which waited for: 5 -> 4; matrix products, arithmetic and copies ran while one was open for 0% -> 0% of each run, Pallas kernels for 4% -> 2%
where the time goes in v1:
time: 100 us; the launch traced here: 99.7 us
  blocking collectives  70 us (70%)
  starting transfers between devices  11 us (11%)
  Pallas kernels  10.3 us (10%)
  waiting for transfers between devices  6.6 us (7%)
    all_to_all x5, blocking collectives, exchange(): return lax.all_to_all(blocks, axis, split_axis=0, concat_axis=0, tiled=True)  70 us
    pallas_call x9, Pallas kernels, call(): pl.pallas_call(body, out_shape=outs, in_specs=specs or [VMEM] * len(args)...  10.3 us
    ppermute x4, starting transfers between devices, by_heads(): lax.ppermute(chunk, 'blk', [(b, (b + inverse * j) % n) for b in range(n)])  6.82 us
    ppermute x4, waiting for transfers between devices, by_heads(): lax.ppermute(chunk, 'blk', [(b, (b + inverse * j) % n) for b in range(n)])  6.58 us
    ppermute x1, starting transfers between devices, per_device(): held_qkv = lax.ppermute(sent_qkv, 'section', [(0, 0)])  2.64 us
  transfers between devices with their start and end apart: 11, of which 4 were waited for; matrix products, arithmetic and copies ran while one was open for 0% of the time, Pallas kernels for 2%

profile of v1, /device:TPU:0, one launch (start us, length us, event | category | flops | bytes accessed | tf_op | source)
XLA Modules:
  0.0 99.7 jit_solution(1081305824246032768)
XLA Ops:
  0.0 0.0 copy-start
  0.0 0.5 collective-permute-start
  0.5 0.1 collective-permute-start.1
  1.2 0.3 copy-done
  1.5 0.5 collective-permute-start.2
  2.0 0.1 collective-permute-start.3
  2.0 0.0 collective-permute-done.other_keys
  2.0 0.0 copy-start.5
  2.0 0.0 collective-permute-done.1.other_values
  2.0 0.0 copy-start.6
  2.0 0.6 copy-done.5
  2.6 0.0 copy-done.6
  2.6 1.9 %shard_map.91 = bf16[16,4,3072]{2,1,0:T(4,128)(2,1)} custom-call(bf16[3,2,3072]{2,1,0:T(2,128)(2,1)} %bitcast.28, bf16[3,2,3072]{2,1,0:T(2,128)(2,1)} %bitcast.30, bf16[3,2,3072]{2,1,0:T(2,128)(2,1)} %bitcast.32, bf16[3,2,3072]{2,1,0:T(2,128)(2,1)} %copy-done.5, bf16[3,2,3072]{2,1,0:T(2,128)(2,1)} %copy-done.6), custom_call_target="tpu_custom_call" | custom-call | bytes 1000000 | tf_op jit(solution)/shard_map/pallas_call | solution.py:135
  4.5 0.0 collective-permute-done.3.other_fresh
  4.5 0.0 collective-permute-done.2.other_mod
  4.6 0.5 collective-permute-start.5
  5.1 2.6 %collective-permute-start.4 = (bf16[576,3072]{1,0:T(8,128)(2,1)}, bf16[576,3072]{1,0:T(8,128)(2,1)S(1)}, u32[]{:S(2)}, u32[]{:S(2)}) collective-permute-start(bf16[576,3072]{1,0:T(8,128)(2,1)} %bitcast.26), channel_id=1, source_target_pairs={{0,0},{1,1},{2,2},{3,3},{4,4},{5,5},{6,6},{7,7},{8,8},{9,9},{10,10... | collective-permute-start | bytes 10616840 | tf_op jit(solution)/shard_map/ppermute | solution.py:448
  7.7 0.0 collective-permute-start.6
  7.7 21.1 %all_to_all.25.arrived = bf16[16,4,3072]{2,1,0:T(4,128)(2,1)S(1)} all-to-all(bf16[16,4,3072]{2,1,0:T(4,128)(2,1)} %shard_map.91), channel_id=1, replica_groups=mesh['section'=2,'blk'=16] {'blk'}, dimensions={0} | all-to-all | bytes 786432 | tf_op jit(solution)/shard_map/all_to_all | solution.py:387
  28.8 0.0 copy-start.3
  28.8 0.0 collective-permute-done.6.other_out.other
  28.8 0.0 collective-permute-done.5.other
  28.8 0.0 collective-permute-done.4.own
  28.8 1.7 %shard_map.92 = (bf16[72,128]{1,0:T(8,128)(2,1)S(1)}, bf16[72,128]{1,0:T(8,128)(2,1)S(1)}, bf16[72,128]{1,0:T(8,128)(2,1)S(1)}, bf16[48,192]{1,0:T(8,128)(2,1)S(1)}) custom-call(bf16[16,4,3072]{2,1,0:T(4,128)(2,1)S(1)} %all_to_all.25.arrived, bf16[576,3072]{1,0:T(8,128)(2,1)S(1)} %collective-permute-done.4.own, ...), custom_call_target="tpu_custom_call" | custom-call | flops 169869312 | bytes 4718592 | tf_op jit(solution)/shard_map/pallas_call | solution.py:135
  30.5 0.9 collective-permute-start.7
  31.5 2.0 %collective-permute-start.8 = (bf16[72,128]{1,0:T(8,128)(2,1)S(1)}, bf16[72,128]{1,0:T(8,128)(2,1)S(1)}, u32[]{:S(2)}, u32[]{:S(2)}) collective-permute-start(bf16[72,128]{1,0:T(8,128)(2,1)S(1)} %get-tuple-element.29), channel_id=1, source_target_pairs={{0,6},{1,7},{2,8},{3,9},{4,10},{5,11},{6,12},{7,13},{8,14},{9,15},... | collective-permute-start | bytes 55304 | tf_op jit(solution)/shard_map/ppermute | solution.py:397
  33.5 0.1 shard_map.93.old
  33.6 1.6 %collective-permute-done.7.chunk1 = bf16[72,128]{1,0:T(8,128)(2,1)S(1)} collective-permute-done((bf16[72,128]{1,0:T(8,128)(2,1)S(1)}, bf16[72,128]{1,0:T(8,128)(2,1)S(1)}, u32[]{:S(2)}, u32[]{:S(2)}) %collective-permute-start.7) | collective-permute-done | bytes 18464 | tf_op jit(solution)/shard_map/ppermute | solution.py:397
  35.2 1.8 %collective-permute-done.8.chunk2 = bf16[72,128]{1,0:T(8,128)(2,1)S(1)} collective-permute-done((bf16[72,128]{1,0:T(8,128)(2,1)S(1)}, bf16[72,128]{1,0:T(8,128)(2,1)S(1)}, u32[]{:S(2)}, u32[]{:S(2)}) %collective-permute-start.8) | collective-permute-done | bytes 18464 | tf_op jit(solution)/shard_map/ppermute | solution.py:397
  37.0 0.0 copy-done.3
  37.0 0.0 copy-done.4
  37.0 1.3 %shard_map.94 = bf16[16,72,128]{2,1,0:T(8,128)(2,1)S(1)} custom-call(bf16[72,128]{1,0:T(8,128)(2,1)S(1)} %get-tuple-element.26.chunk0, bf16[72,128]{1,0:T(8,128)(2,1)S(1)} %collective-permute-done.7.chunk1, bf16[72,128]{1,0:T(8,128)(2,1)S(1)} %collective-permute-done.8.chunk2, bf16[2,48,384]{2,1,0:T(8,128)(2,1)S(1)} %shard_map.93.old, ...), custom_call_target="tpu_custom_call" | custom-call | flops 3538944 | bytes 300000 | tf_op jit(solution)/shard_map/pallas_call | solution.py:135
  38.3 0.0 copy-start.2
  38.3 14.0 %all_to_all.26.blocks = bf16[16,72,128]{2,1,0:T(8,128)(2,1)S(1)} all-to-all(bf16[16,72,128]{2,1,0:T(8,128)(2,1)S(1)} %shard_map.94), channel_id=1, replica_groups=mesh['section'=2,'blk'=16] {'blk'}, dimensions={0} | all-to-all | bytes 589824 | tf_op jit(solution)/shard_map/all_to_all | solution.py:387
  52.3 0.0 copy-done.1
  52.3 0.9 shard_map.95
  53.2 12.2 %all_to_all.27.blocks = bf16[16,72,128]{2,1,0:T(8,128)(2,1)S(1)} all-to-all(bf16[16,72,128]{2,1,0:T(8,128)(2,1)S(1)} %get-tuple-element.33), channel_id=1, replica_groups=mesh['section'=2,'blk'=16] {'blk'}, dimensions={0} | all-to-all | bytes 589824 | tf_op jit(solution)/shard_map/all_to_all | solution.py:387
  65.4 0.0 copy-done.2
  65.4 1.7 %shard_map.96 = (bf16[72,128]{1,0:T(8,128)(2,1)S(1)}, bf16[72,128]{1,0:T(8,128)(2,1)S(1)}, bf16[72,128]{1,0:T(8,128)(2,1)S(1)}, bf16[48,192]{1,0:T(8,128)(2,1)S(1)}) custom-call(bf16[16,72,128]{2,1,0:T(8,128)(2,1)S(1)} %all_to_all.27.blocks, bf16[576,3072]{1,0:T(8,128)(2,1)S(1)} %bitcast.27, bf16[576,3072]{1,0:T(8,128)(2,1)S(1)} %collective-permute-done.5.other, ...), custom_call_target="tpu_custom_call" | custom-call | flops 169869312 | bytes 4718592 | tf_op jit(solution)/shard_map/pallas_call | solution.py:135
  67.1 1.5 %collective-permute-start.9 = (bf16[72,128]{1,0:T(8,128)(2,1)S(1)}, bf16[72,128]{1,0:T(8,128)(2,1)S(1)}, u32[]{:S(2)}, u32[]{:S(2)}) collective-permute-start(bf16[72,128]{1,0:T(8,128)(2,1)S(1)} %get-tuple-element.35), channel_id=1, source_target_pairs={{0,11},{1,12},{2,13},{3,14},{4,15},{5,0},{6,1},{7,2},{8,3},{9,4},{... | collective-permute-start | bytes 55304 | tf_op jit(solution)/shard_map/ppermute | solution.py:397
  68.5 2.4 %collective-permute-start.10 = (bf16[72,128]{1,0:T(8,128)(2,1)S(1)}, bf16[72,128]{1,0:T(8,128)(2,1)S(1)}, u32[]{:S(2)}, u32[]{:S(2)}) collective-permute-start(bf16[72,128]{1,0:T(8,128)(2,1)S(1)} %get-tuple-element.36), channel_id=1, source_target_pairs={{0,6},{1,7},{2,8},{3,9},{4,10},{5,11},{6,12},{7,13},{8,14},{9,15},... | collective-permute-start | bytes 55304 | tf_op jit(solution)/shard_map/ppermute | solution.py:397
  71.0 0.8 collective-permute-done.9.chunk1
  71.7 2.4 %collective-permute-done.10.chunk2 = bf16[72,128]{1,0:T(8,128)(2,1)S(1)} collective-permute-done((bf16[72,128]{1,0:T(8,128)(2,1)S(1)}, bf16[72,128]{1,0:T(8,128)(2,1)S(1)}, u32[]{:S(2)}, u32[]{:S(2)}) %collective-permute-start.10) | collective-permute-done | bytes 18464 | tf_op jit(solution)/shard_map/ppermute | solution.py:397
  74.1 1.3 %shard_map.97 = bf16[16,72,128]{2,1,0:T(8,128)(2,1)S(1)} custom-call(bf16[72,128]{1,0:T(8,128)(2,1)S(1)} %get-tuple-element.34.chunk0, bf16[72,128]{1,0:T(8,128)(2,1)S(1)} %collective-permute-done.9.chunk1, bf16[72,128]{1,0:T(8,128)(2,1)S(1)} %collective-permute-done.10.chunk2, bf16[2,48,384]{2,1,0:T(8,128)(2,1)S(1)} %shard_map.93.old, ...), custom_call_target="tpu_custom_call" | custom-call | flops 3538944 | bytes 300000 | tf_op jit(solution)/shard_map/pallas_call | solution.py:135
  75.4 13.1 %all_to_all.28.blocks = bf16[16,72,128]{2,1,0:T(8,128)(2,1)S(1)} all-to-all(bf16[16,72,128]{2,1,0:T(8,128)(2,1)S(1)} %shard_map.97), channel_id=1, replica_groups=mesh['section'=2,'blk'=16] {'blk'}, dimensions={0} | all-to-all | bytes 589824 | tf_op jit(solution)/shard_map/all_to_all | solution.py:387
  88.5 0.7 shard_map.98
  89.2 9.7 %all_to_all.29.arrived = bf16[32,4,192]{2,1,0:T(4,128)(2,1)S(1)} all-to-all(bf16[32,4,192]{2,1,0:T(4,128)(2,1)S(1)} %shard_map.98), channel_id=1, replica_groups=mesh['section'=2,'blk'=16] {'section','blk'}, dimensions={0} | all-to-all | bytes 98304 | tf_op jit(solution)/shard_map/all_to_all | solution.py:387
  98.9 0.8 shard_map.99
  (3 shorter events, 0.0 us)
Async XLA Ops:
  0.0 1.5 %copy-start = (f32[1,50,3,3072]{3,0,2,1:T(1,128)S(1)}, f32[1,50,3,3072]{3,0,2,1:T(1,128)}, u32[]{:S(2)}) copy-start(f32[1,50,3,3072]{3,0,2,1:T(1,128)} %param.12) | copy-start | bytes 5529604
  0.0 2.0 %collective-permute-start = (bf16[3,2,3072]{2,1,0:T(2,128)(2,1)}, bf16[3,2,3072]{2,1,0:T(2,128)(2,1)S(1)}, u32[]{:S(2)}, u32[]{:S(2)}) collective-permute-start(bf16[3,2,3072]{2,1,0:T(2,128)(2,1)} %bitcast.29), channel_id=1, source_target_pairs={{0,16},{16,0},{1,17},{17,1},{2,18},{18,2},{3,19},{19,3},{4,20},{20... | collective-permute-start | bytes 110600 | tf_op jit(solution)/shard_map/ppermute | solution.py:391
  0.5 1.6 %collective-permute-start.1 = (bf16[3,2,3072]{2,1,0:T(2,128)(2,1)}, bf16[3,2,3072]{2,1,0:T(2,128)(2,1)S(1)}, u32[]{:S(2)}, u32[]{:S(2)}) collective-permute-start(bf16[3,2,3072]{2,1,0:T(2,128)(2,1)} %bitcast.31), channel_id=1, source_target_pairs={{0,16},{16,0},{1,17},{17,1},{2,18},{18,2},{3,19},{19,3},{4,20},{20... | collective-permute-start | bytes 110600 | tf_op jit(solution)/shard_map/ppermute | solution.py:391
  1.5 3.0 %collective-permute-start.2 = (f32[3,1,3072]{2,1,0:T(1,128)S(1)}, f32[3,1,3072]{2,1,0:T(1,128)S(1)}, u32[]{:S(2)}, u32[]{:S(2)}) collective-permute-start(f32[3,1,3072]{2,1,0:T(1,128)S(1)} %dynamic-slice_bitcast_fusion.mod), channel_id=1, source_target_pairs={{0,16},{16,0},{1,17},{17,1},{2,18},{18,2},{3,19},{19,3},{4,20},{20... | collective-permute-start | bytes 110600 | tf_op jit(solution)/shard_map/ppermute | solution.py:391
  2.0 2.6 %collective-permute-start.3 = (s32[1,2,16]{2,1,0:T(2,128)}, s32[1,2,16]{2,1,0:T(2,128)S(1)}, u32[]{:S(2)}, u32[]{:S(2)}) collective-permute-start(s32[1,2,16]{2,1,0:T(2,128)} %fresh.3), channel_id=1, source_target_pairs={{0,16},{16,0},{1,17},{17,1},{2,18},{18,2},{3,19},{19,3},{4,20},{20... | collective-permute-start | bytes 392 | tf_op jit(solution)/shard_map/ppermute | solution.py:391
  2.0 0.6 copy-start.5
  2.0 0.6 copy-start.6
  4.6 24.2 %collective-permute-start.5 = (bf16[576,3072]{1,0:T(8,128)(2,1)}, bf16[576,3072]{1,0:T(8,128)(2,1)S(1)}, u32[]{:S(2)}, u32[]{:S(2)}) collective-permute-start(bf16[576,3072]{1,0:T(8,128)(2,1)} %bitcast.25), channel_id=1, source_target_pairs={{0,16},{16,0},{1,17},{17,1},{2,18},{18,2},{3,19},{19,3},{4,20},{20... | collective-permute-start | bytes 10616840 | tf_op jit(solution)/shard_map/ppermute | solution.py:391
  5.1 23.7 %collective-permute-start.4 = (bf16[576,3072]{1,0:T(8,128)(2,1)}, bf16[576,3072]{1,0:T(8,128)(2,1)S(1)}, u32[]{:S(2)}, u32[]{:S(2)}) collective-permute-start(bf16[576,3072]{1,0:T(8,128)(2,1)} %bitcast.26), channel_id=1, source_target_pairs={{0,0},{1,1},{2,2},{3,3},{4,4},{5,5},{6,6},{7,7},{8,8},{9,9},{10,10... | collective-permute-start | bytes 10616840 | tf_op jit(solution)/shard_map/ppermute | solution.py:448
  7.7 21.1 %collective-permute-start.6 = (bf16[192,3072]{1,0:T(8,128)(2,1)}, bf16[192,3072]{1,0:T(8,128)(2,1)S(1)}, u32[]{:S(2)}, u32[]{:S(2)}) collective-permute-start(bf16[192,3072]{1,0:T(8,128)(2,1)} %bitcast.22), channel_id=1, source_target_pairs={{0,16},{16,0},{1,17},{17,1},{2,18},{18,2},{3,19},{19,3},{4,20},{20... | collective-permute-start | bytes 3538952 | tf_op jit(solution)/shard_map/ppermute | solution.py:391
  28.8 8.3 %copy-start.3 = (s32[1,2,16]{2,1,0:T(2,128)S(1)}, s32[1,2,16]{2,1,0:T(2,128)}, u32[]{:S(2)}) copy-start(s32[1,2,16]{2,1,0:T(2,128)} %fresh.3) | copy-start | bytes 388
  28.8 8.3 %copy-start.4 = (s32[2,16]{1,0:T(2,128)S(1)}, s32[2,16]{1,0:T(2,128)}, u32[]{:S(2)}) copy-start(s32[2,16]{1,0:T(2,128)} %live.3) | copy-start | bytes 388
  30.5 21.8 %copy-start.1 = (bf16[1,3072,192]{1,2,0:T(8,128)(2,1)S(1)}, bf16[1,3072,192]{1,2,0:T(8,128)(2,1)}, u32[]{:S(2)}) copy-start(bf16[1,3072,192]{1,2,0:T(8,128)(2,1)} %param.11) | copy-start | bytes 3538948
  30.5 4.7 %collective-permute-start.7 = (bf16[72,128]{1,0:T(8,128)(2,1)S(1)}, bf16[72,128]{1,0:T(8,128)(2,1)S(1)}, u32[]{:S(2)}, u32[]{:S(2)}) collective-permute-start(bf16[72,128]{1,0:T(8,128)(2,1)S(1)} %get-tuple-element.28), channel_id=1, source_target_pairs={{0,11},{1,12},{2,13},{3,14},{4,15},{5,0},{6,1},{7,2},{8,3},{9,4},{... | collective-permute-start | bytes 55304 | tf_op jit(solution)/shard_map/ppermute | solution.py:397
  31.5 5.6 %collective-permute-start.8 = (bf16[72,128]{1,0:T(8,128)(2,1)S(1)}, bf16[72,128]{1,0:T(8,128)(2,1)S(1)}, u32[]{:S(2)}, u32[]{:S(2)}) collective-permute-start(bf16[72,128]{1,0:T(8,128)(2,1)S(1)} %get-tuple-element.29), channel_id=1, source_target_pairs={{0,6},{1,7},{2,8},{3,9},{4,10},{5,11},{6,12},{7,13},{8,14},{9,15},... | collective-permute-start | bytes 55304 | tf_op jit(solution)/shard_map/ppermute | solution.py:397
  38.3 27.0 %copy-start.2 = (bf16[1,3072,576]{1,2,0:T(8,128)(2,1)S(1)}, bf16[1,3072,576]{1,2,0:T(8,128)(2,1)}, u32[]{:S(2)}) copy-start(bf16[1,3072,576]{1,2,0:T(8,128)(2,1)} %param.10) | copy-start | bytes 10616836
  67.1 4.7 %collective-permute-start.9 = (bf16[72,128]{1,0:T(8,128)(2,1)S(1)}, bf16[72,128]{1,0:T(8,128)(2,1)S(1)}, u32[]{:S(2)}, u32[]{:S(2)}) collective-permute-start(bf16[72,128]{1,0:T(8,128)(2,1)S(1)} %get-tuple-element.35), channel_id=1, source_target_pairs={{0,11},{1,12},{2,13},{3,14},{4,15},{5,0},{6,1},{7,2},{8,3},{9,4},{... | collective-permute-start | bytes 55304 | tf_op jit(solution)/shard_map/ppermute | solution.py:397
  68.5 5.6 %collective-permute-start.10 = (bf16[72,128]{1,0:T(8,128)(2,1)S(1)}, bf16[72,128]{1,0:T(8,128)(2,1)S(1)}, u32[]{:S(2)}, u32[]{:S(2)}) collective-permute-start(bf16[72,128]{1,0:T(8,128)(2,1)S(1)} %get-tuple-element.36), channel_id=1, source_target_pairs={{0,6},{1,7},{2,8},{3,9},{4,10},{5,11},{6,12},{7,13},{8,14},{9,15},... | collective-permute-start | bytes 55304 | tf_op jit(solution)/shard_map/ppermute | solution.py:397

commit v2 on v1

--- a/solution.py
+++ b/solution.py
@@ -240,21 +240,44 @@
         chunk[...] = pack(columns[:, 192 * j : 192 * j + 192])
 
 
-def first_projection(arrived, own, other, mod, other_mod, other_out, chunk0, chunk1, chunk2, residual, stream, scales, normed, columns):
+def fetch(layer, own, other, here, sems):
+    parts = sems.shape[0]
+    size = here.shape[0] // parts
+
+    def copies(source):
+        for i in range(parts):
+            at = pl.ds(i * size, size)
+            yield pltpu.make_async_copy(source.at[at], here.at[at], sems.at[i])
+
+    def start(source):
+        for copy in copies(source):
+            copy.start()
+
+    def wait():
+        for copy in copies(own):
+            copy.wait()
+
+    held = lax.axis_index("section") == layer
+    pl.when(held)(lambda: start(own))
+    pl.when(jnp.logical_not(held))(lambda: start(other))
+    return wait
+
+
+def first_projection(arrived, own, other, mod, other_mod, other_out, chunk0, chunk1, chunk2, residual, stream, scales, normed, weight, sems):
+    wait = fetch(0, own, other, weight, sems)
     n = arrived.shape[0]
     rows = stream.shape[0] // n
     for b in range(n):
         stream[rows * b : rows * b + rows, :] = arrived[b, :rows, :].astype(F32)
     normalise(0, stream, mod, other_mod, normed, residual, scales)
-    dot_into(0, normed, own, other, columns)
-    chunks_of(columns, (chunk0, chunk1, chunk2))
-
-
-def next_projection(blocks, own, other, mod, other_mod, chunk0, chunk1, chunk2, residual, stream, scales, normed, columns):
+    wait()
+    chunks_of(dot_nt(normed[...], weight[...]).astype(BF16), (chunk0, chunk1, chunk2))
+
+
+def next_projection(blocks, weight, mod, other_mod, chunk0, chunk1, chunk2, residual, stream, scales, normed):
     assemble(blocks, stream)
     normalise(1, stream, mod, other_mod, normed, residual, scales)
-    dot_into(1, normed, own, other, columns)
-    chunks_of(columns, (chunk0, chunk1, chunk2))
+    chunks_of(dot_nt(normed[...], weight[...]).astype(BF16), (chunk0, chunk1, chunk2))
 
 
 def attention(layer, chunk0, chunk1, chunk2, old, fresh, other_fresh, live, attn):
@@ -360,7 +383,8 @@
             leaving[b, rows : rows + 1, i * 4 * columns : (i + 1) * 4 * columns] = block[i : i + 1].astype(BF16)
 
 
-def stale_by_token(arrived, old, rows):
+def settle(arrived, own, other, old, weight, rows, sems):
+    wait = fetch(1, own, other, weight, sems)
     n = arrived.shape[0]
     per = rows.shape[1] // n
     wide = rows.shape[2]
@@ -371,6 +395,7 @@
                 at = (i * 2 + layer) * wide
                 rows[layer, per * b + i : per * b + i + 1, :] = flat[:, at : at + wide]
     old[...] = rows[...].astype(BF16)
+    wait()
 
 
 def to_rows(arrived, out, rows):
@@ -425,6 +450,12 @@
     old_keys = jnp.transpose(k_stale[0], (1, 0, 2))
     old_values = jnp.transpose(v_stale[0], (1, 0, 2))
 
+    small = [swap_sections(array) for array in (old_keys, old_values, mod, fresh)]
+    (other_keys, other_values, other_mod, other_fresh), sent_qkv, sent_out = lax.optimization_barrier(
+        (small, own_qkv, own_out)
+    )
+    other_qkv, other_out = swap_sections(sent_qkv), swap_sections(sent_out)
+    out = (own_out, other_out)
     leaving = call(
         first_exchange,
         shape((n, 4, width), BF16),
@@ -433,46 +464,52 @@
         jnp.transpose(hidden, (1, 0, 2)),
         old_keys,
         old_values,
-        swap_sections(old_keys),
-        swap_sections(old_values),
+        other_keys,
+        other_values,
         specs=[HBM] * 3 + [ANY] * 2,
         spare=4 << 20,
     )
-    leaving, other_mod, other_fresh, sent_qkv, sent_out = lax.optimization_barrier(
-        (leaving, swap_sections(mod), swap_sections(fresh), own_qkv, own_out)
-    )
     mods = (mod, other_mod)
     flags = (fresh, other_fresh)
-    other_qkv, other_out = swap_sections(sent_qkv), swap_sections(sent_out)
-    out = (own_out, other_out)
-    held_qkv = lax.ppermute(sent_qkv, "section", [(0, 0)])
     arrived = exchange(leaving, "blk")
 
     blocks = arrived
     for layer in range(2):
-        *chunks, residual = call(
-            next_projection if layer else first_projection,
-            [packed, packed, packed, cols],
-            [
-                pltpu.VMEM((tokens, width), F32),
-                pltpu.VMEM(mod.shape, F32),
-                pltpu.VMEM((tokens, width), BF16),
-                pltpu.VMEM((tokens, 3 * columns), BF16),
-            ],
-            (2 * tokens * width * 3 * columns, 8 * width * columns),
-            blocks,
-            *((own_qkv, other_qkv, *mods) if layer else (held_qkv, other_qkv, *mods, other_out)),
-            **({} if layer else {"specs": [VMEM] * 5 + [ANY]}),
-        )
+        scratch = [
+            pltpu.VMEM((tokens, width), F32),
+            pltpu.VMEM(mod.shape, F32),
+            pltpu.VMEM((tokens, width), BF16),
+        ]
+        outs = [packed, packed, packed, cols]
+        cost = (2 * tokens * width * 3 * columns, 8 * width * columns)
+        sems = pltpu.SemaphoreType.DMA((36,))
         if layer == 0:
+            *chunks, residual = call(
+                first_projection,
+                outs,
+                scratch + [pltpu.VMEM(own_qkv.shape, BF16), sems],
+                cost,
+                blocks,
+                own_qkv,
+                other_qkv,
+                *mods,
+                other_out,
+                specs=[VMEM, HBM, ANY, VMEM, VMEM, ANY],
+                spare=12 << 20,
+            )
             arrived, chunks[1] = lax.optimization_barrier((arrived, chunks[1]))
-            old = call(
-                stale_by_token,
-                shape((2, tokens, 2 * columns), BF16),
-                [pltpu.VMEM((2, tokens, 2 * columns), F32)],
+            old, next_qkv = call(
+                settle,
+                [shape((2, tokens, 2 * columns), BF16), shape(own_qkv.shape, BF16)],
+                [pltpu.VMEM((2, tokens, 2 * columns), F32), sems],
                 (0, 200000),
                 arrived,
+                own_qkv,
+                other_qkv,
+                specs=[VMEM, HBM, ANY],
             )
+        else:
+            *chunks, residual = call(next_projection, outs, scratch, cost, blocks, next_qkv, *mods)
         attn = call(
             functools.partial(attention, layer),
             copies,

time: 100 us -> 104 us (1.040)
  blocking collectives: 70 us -> 74.2 us
  Pallas kernels: 10.3 us -> 14.5 us
  starting transfers between devices: 11 us -> 7.51 us
    all_to_all x5, blocking collectives: 70 us -> 74.2 us  [exchange(): return lax.all_to_all(blocks, axis, split_axis=0, concat_axis=0, tiled=True)]
    pallas_call x9, Pallas kernels: 10.3 us -> 14.5 us  [call(): pl.pallas_call(body, out_shape=outs, in_specs=specs or [VMEM] * len(args)...]
    ppermute x1 -> x0, starting transfers between devices: 2.64 us -> none  [per_device(): held_qkv = lax.ppermute(sent_qkv, 'section', [(0, 0)])]
    ppermute x4, waiting for transfers between devices: 6.58 us -> 4.58 us  [by_heads(): lax.ppermute(chunk, 'blk', [(b, (b + inverse * j) % n) for b in range(n)])]
    ppermute x6, waiting for transfers between devices: 0.02 us -> 1.31 us  [swap_sections(): return lax.ppermute(array, 'section', [(0, 1), (1, 0)])]
  transfers between devices with their start and end apart: 11 -> 10, of which waited for: 4 -> 4; matrix products, arithmetic and copies ran while one was open for 0% -> 0% of each run, Pallas kernels for 2% -> 4%
where the time goes in v2:
time: 104 us
  blocking collectives  74.2 us (71%)
  Pallas kernels  14.5 us (14%)
  starting transfers between devices  7.51 us (7%)
  waiting for transfers between devices  5.88 us (6%)
    all_to_all x5, blocking collectives, exchange(): return lax.all_to_all(blocks, axis, split_axis=0, concat_axis=0, tiled=True)  74.2 us
    pallas_call x9, Pallas kernels, call(): pl.pallas_call(body, out_shape=outs, in_specs=specs or [VMEM] * len(args)...  14.5 us
    ppermute x4, starting transfers between devices, by_heads(): lax.ppermute(chunk, 'blk', [(b, (b + inverse * j) % n) for b in range(n)])  5.91 us
    ppermute x4, waiting for transfers between devices, by_heads(): lax.ppermute(chunk, 'blk', [(b, (b + inverse * j) % n) for b in range(n)])  4.58 us
  transfers between devices with their start and end apart: 10, of which 4 were waited for; matrix products, arithmetic and copies ran while one was open for 0% of the time, Pallas kernels for 4%

profile of v2, /device:TPU:0, one launch (start us, length us, event | category | flops | bytes accessed | tf_op | source)
XLA Modules:
  0.0 103.8 jit_solution(558141855030597368)
XLA Ops:
  0.0 0.0 copy-start
  0.8 0.7 copy-done
  1.5 0.5 collective-permute-start.2
  2.0 0.1 collective-permute-start
  2.0 0.5 collective-permute-start.1
  2.5 0.1 collective-permute-start.3
  2.5 1.3 %collective-permute-done.3.other_fresh = s32[1,2,16]{2,1,0:T(2,128)S(1)} collective-permute-done((s32[1,2,16]{2,1,0:T(2,128)}, s32[1,2,16]{2,1,0:T(2,128)S(1)}, u32[]{:S(2)}, u32[]{:S(2)}) %collective-permute-start.3) | collective-permute-done | bytes 160 | tf_op jit(solution)/shard_map/ppermute | solution.py:416
  3.8 0.0 collective-permute-done.2.other_mod
  3.8 0.0 collective-permute-done.other_keys
  3.8 0.0 copy-start.5
  3.8 0.0 collective-permute-done.1.other_values
  3.9 0.0 copy-start.6
  3.9 0.2 collective-permute-start.4
  4.1 0.3 collective-permute-start.5
  4.4 0.0 copy-done.5
  4.5 0.0 copy-done.6
  4.5 1.9 %shard_map.91 = bf16[16,4,3072]{2,1,0:T(4,128)(2,1)} custom-call(bf16[3,2,3072]{2,1,0:T(2,128)(2,1)} %bitcast.28, bf16[3,2,3072]{2,1,0:T(2,128)(2,1)} %bitcast.30, bf16[3,2,3072]{2,1,0:T(2,128)(2,1)} %bitcast.32, bf16[3,2,3072]{2,1,0:T(2,128)(2,1)} %copy-done.5, bf16[3,2,3072]{2,1,0:T(2,128)(2,1)} %copy-done.6), custom_call_target="tpu_custom_call" | custom-call | bytes 1000000 | tf_op jit(solution)/shard_map/pallas_call | solution.py:135
  6.3 21.1 %all_to_all.25.arrived = bf16[16,4,3072]{2,1,0:T(4,128)(2,1)S(1)} all-to-all(bf16[16,4,3072]{2,1,0:T(4,128)(2,1)} %shard_map.91), channel_id=1, replica_groups=mesh['section'=2,'blk'=16] {'blk'}, dimensions={0} | all-to-all | bytes 786432 | tf_op jit(solution)/shard_map/all_to_all | solution.py:412
  27.5 0.0 collective-permute-done.5.other_out.other
  27.5 0.0 collective-permute-done.4.other
  27.5 0.0 copy-start.1
  27.5 3.8 %shard_map.92 = (bf16[72,128]{1,0:T(8,128)(2,1)S(1)}, bf16[72,128]{1,0:T(8,128)(2,1)S(1)}, bf16[72,128]{1,0:T(8,128)(2,1)S(1)}, bf16[48,192]{1,0:T(8,128)(2,1)S(1)}) custom-call(bf16[16,4,3072]{2,1,0:T(4,128)(2,1)S(1)} %all_to_all.25.arrived, bf16[576,3072]{1,0:T(8,128)(2,1)} %bitcast.23, bf16[576,3072]{1,0:T(8,128)(2,1)} %collective-permute-done.4.other, ...), custom_call_target="tpu_custom_call" | custom-call | flops 169869312 | bytes 4718592 | tf_op jit(solution)/shard_map/pallas_call | solution.py:135
  31.3 0.9 collective-permute-start.6
  32.2 0.0 copy-start.3
  32.2 0.0 copy-start.4
  32.2 0.0 copy-start.2
  32.2 2.1 %collective-permute-start.7 = (bf16[72,128]{1,0:T(8,128)(2,1)S(1)}, bf16[72,128]{1,0:T(8,128)(2,1)S(1)}, u32[]{:S(2)}, u32[]{:S(2)}) collective-permute-start(bf16[72,128]{1,0:T(8,128)(2,1)S(1)} %get-tuple-element.33), channel_id=1, source_target_pairs={{0,6},{1,7},{2,8},{3,9},{4,10},{5,11},{6,12},{7,13},{8,14},{9,15},... | collective-permute-start | bytes 55304 | tf_op jit(solution)/shard_map/ppermute | solution.py:422
  34.3 0.0 copy-done.1
  34.3 2.4 %shard_map.93 = (bf16[2,48,384]{2,1,0:T(8,128)(2,1)S(1)}, bf16[576,3072]{1,0:T(8,128)(2,1)S(1)}) custom-call(bf16[16,4,3072]{2,1,0:T(4,128)(2,1)S(1)} %all_to_all.25.arrived, bf16[576,3072]{1,0:T(8,128)(2,1)S(1)} %bitcast.24, bf16[576,3072]{1,0:T(8,128)(2,1)} %collective-permute-done.4.other), custom_call_target="tpu_custom_call" | custom-call | bytes 200000 | tf_op jit(solution)/shard_map/pallas_call | solution.py:135
  36.7 0.0 collective-permute-done.6.chunk1
  36.7 1.1 %collective-permute-done.7.chunk2 = bf16[72,128]{1,0:T(8,128)(2,1)S(1)} collective-permute-done((bf16[72,128]{1,0:T(8,128)(2,1)S(1)}, bf16[72,128]{1,0:T(8,128)(2,1)S(1)}, u32[]{:S(2)}, u32[]{:S(2)}) %collective-permute-start.7) | collective-permute-done | bytes 18464 | tf_op jit(solution)/shard_map/ppermute | solution.py:422
  37.7 0.0 copy-done.3
  37.7 0.0 copy-done.4
  37.7 1.3 %shard_map.94 = bf16[16,72,128]{2,1,0:T(8,128)(2,1)S(1)} custom-call(bf16[72,128]{1,0:T(8,128)(2,1)S(1)} %get-tuple-element.30.chunk0, bf16[72,128]{1,0:T(8,128)(2,1)S(1)} %collective-permute-done.6.chunk1, bf16[72,128]{1,0:T(8,128)(2,1)S(1)} %collective-permute-done.7.chunk2, bf16[2,48,384]{2,1,0:T(8,128)(2,1)S(1)} %get-tuple-element.35.old, ...), custom_call_target="tpu_custom_call" | custom-call | flops 3538944 | bytes 300000 | tf_op jit(solution)/shard_map/pallas_call | solution.py:135
  39.0 16.4 %all_to_all.26.blocks = bf16[16,72,128]{2,1,0:T(8,128)(2,1)S(1)} all-to-all(bf16[16,72,128]{2,1,0:T(8,128)(2,1)S(1)} %shard_map.94), channel_id=1, replica_groups=mesh['section'=2,'blk'=16] {'blk'}, dimensions={0} | all-to-all | bytes 589824 | tf_op jit(solution)/shard_map/all_to_all | solution.py:412
  55.4 0.0 copy-done.2
  55.4 0.9 shard_map.95
  56.3 13.5 %all_to_all.27.blocks = bf16[16,72,128]{2,1,0:T(8,128)(2,1)S(1)} all-to-all(bf16[16,72,128]{2,1,0:T(8,128)(2,1)S(1)} %get-tuple-element.38), channel_id=1, replica_groups=mesh['section'=2,'blk'=16] {'blk'}, dimensions={0} | all-to-all | bytes 589824 | tf_op jit(solution)/shard_map/all_to_all | solution.py:412
  69.8 1.6 %shard_map.96 = (bf16[72,128]{1,0:T(8,128)(2,1)S(1)}, bf16[72,128]{1,0:T(8,128)(2,1)S(1)}, bf16[72,128]{1,0:T(8,128)(2,1)S(1)}, bf16[48,192]{1,0:T(8,128)(2,1)S(1)}) custom-call(bf16[16,72,128]{2,1,0:T(8,128)(2,1)S(1)} %all_to_all.27.blocks, bf16[576,3072]{1,0:T(8,128)(2,1)S(1)} %get-tuple-element.39.weight, ...), custom_call_target="tpu_custom_call" | custom-call | flops 169869312 | bytes 4718592 | tf_op jit(solution)/shard_map/pallas_call | solution.py:135
  71.4 0.9 collective-permute-start.8
  72.2 2.1 %collective-permute-start.9 = (bf16[72,128]{1,0:T(8,128)(2,1)S(1)}, bf16[72,128]{1,0:T(8,128)(2,1)S(1)}, u32[]{:S(2)}, u32[]{:S(2)}) collective-permute-start(bf16[72,128]{1,0:T(8,128)(2,1)S(1)} %get-tuple-element.42), channel_id=1, source_target_pairs={{0,6},{1,7},{2,8},{3,9},{4,10},{5,11},{6,12},{7,13},{8,14},{9,15},... | collective-permute-start | bytes 55304 | tf_op jit(solution)/shard_map/ppermute | solution.py:422
  74.3 1.7 %collective-permute-done.8.chunk1 = bf16[72,128]{1,0:T(8,128)(2,1)S(1)} collective-permute-done((bf16[72,128]{1,0:T(8,128)(2,1)S(1)}, bf16[72,128]{1,0:T(8,128)(2,1)S(1)}, u32[]{:S(2)}, u32[]{:S(2)}) %collective-permute-start.8) | collective-permute-done | bytes 18464 | tf_op jit(solution)/shard_map/ppermute | solution.py:422
  76.0 1.8 %collective-permute-done.9.chunk2 = bf16[72,128]{1,0:T(8,128)(2,1)S(1)} collective-permute-done((bf16[72,128]{1,0:T(8,128)(2,1)S(1)}, bf16[72,128]{1,0:T(8,128)(2,1)S(1)}, u32[]{:S(2)}, u32[]{:S(2)}) %collective-permute-start.9) | collective-permute-done | bytes 18464 | tf_op jit(solution)/shard_map/ppermute | solution.py:422
  77.8 1.3 %shard_map.97 = bf16[16,72,128]{2,1,0:T(8,128)(2,1)S(1)} custom-call(bf16[72,128]{1,0:T(8,128)(2,1)S(1)} %get-tuple-element.40.chunk0, bf16[72,128]{1,0:T(8,128)(2,1)S(1)} %collective-permute-done.8.chunk1, bf16[72,128]{1,0:T(8,128)(2,1)S(1)} %collective-permute-done.9.chunk2, bf16[2,48,384]{2,1,0:T(8,128)(2,1)S(1)} %get-tuple-element.35.old, ...), custom_call_target="tpu_custom_call" | custom-call | flops 3538944 | bytes 300000 | tf_op jit(solution)/shard_map/pallas_call | solution.py:135
  79.1 13.5 %all_to_all.28.blocks = bf16[16,72,128]{2,1,0:T(8,128)(2,1)S(1)} all-to-all(bf16[16,72,128]{2,1,0:T(8,128)(2,1)S(1)} %shard_map.97), channel_id=1, replica_groups=mesh['section'=2,'blk'=16] {'blk'}, dimensions={0} | all-to-all | bytes 589824 | tf_op jit(solution)/shard_map/all_to_all | solution.py:412
  92.6 0.7 shard_map.98
  93.3 9.7 %all_to_all.29.arrived = bf16[32,4,192]{2,1,0:T(4,128)(2,1)S(1)} all-to-all(bf16[32,4,192]{2,1,0:T(4,128)(2,1)S(1)} %shard_map.98), channel_id=1, replica_groups=mesh['section'=2,'blk'=16] {'section','blk'}, dimensions={0} | all-to-all | bytes 98304 | tf_op jit(solution)/shard_map/all_to_all | solution.py:412
  103.0 0.8 shard_map.99
  (1 shorter events, 0.0 us)
Async XLA Ops:
  0.0 1.5 %copy-start = (f32[1,50,3,3072]{3,0,2,1:T(1,128)S(1)}, f32[1,50,3,3072]{3,0,2,1:T(1,128)}, u32[]{:S(2)}) copy-start(f32[1,50,3,3072]{3,0,2,1:T(1,128)} %param.12) | copy-start | bytes 5529604
  1.5 2.3 %collective-permute-start.2 = (f32[3,1,3072]{2,1,0:T(1,128)S(1)}, f32[3,1,3072]{2,1,0:T(1,128)S(1)}, u32[]{:S(2)}, u32[]{:S(2)}) collective-permute-start(f32[3,1,3072]{2,1,0:T(1,128)S(1)} %dynamic-slice_bitcast_fusion.mod), channel_id=1, source_target_pairs={{0,16},{16,0},{1,17},{17,1},{2,18},{18,2},{3,19},{19,3},{4,20},{20... | collective-permute-start | bytes 110600 | tf_op jit(solution)/shard_map/ppermute | solution.py:416
  2.0 1.9 %collective-permute-start = (bf16[3,2,3072]{2,1,0:T(2,128)(2,1)}, bf16[3,2,3072]{2,1,0:T(2,128)(2,1)S(1)}, u32[]{:S(2)}, u32[]{:S(2)}) collective-permute-start(bf16[3,2,3072]{2,1,0:T(2,128)(2,1)} %bitcast.29), channel_id=1, source_target_pairs={{0,16},{16,0},{1,17},{17,1},{2,18},{18,2},{3,19},{19,3},{4,20},{20... | collective-permute-start | bytes 110600 | tf_op jit(solution)/shard_map/ppermute | solution.py:416
  2.0 1.8 %collective-permute-start.1 = (bf16[3,2,3072]{2,1,0:T(2,128)(2,1)}, bf16[3,2,3072]{2,1,0:T(2,128)(2,1)S(1)}, u32[]{:S(2)}, u32[]{:S(2)}) collective-permute-start(bf16[3,2,3072]{2,1,0:T(2,128)(2,1)} %bitcast.31), channel_id=1, source_target_pairs={{0,16},{16,0},{1,17},{17,1},{2,18},{18,2},{3,19},{19,3},{4,20},{20... | collective-permute-start | bytes 110600 | tf_op jit(solution)/shard_map/ppermute | solution.py:416
  2.5 1.4 %collective-permute-start.3 = (s32[1,2,16]{2,1,0:T(2,128)}, s32[1,2,16]{2,1,0:T(2,128)S(1)}, u32[]{:S(2)}, u32[]{:S(2)}) collective-permute-start(s32[1,2,16]{2,1,0:T(2,128)} %fresh.3), channel_id=1, source_target_pairs={{0,16},{16,0},{1,17},{17,1},{2,18},{18,2},{3,19},{19,3},{4,20},{20... | collective-permute-start | bytes 392 | tf_op jit(solution)/shard_map/ppermute | solution.py:416
  3.8 0.6 copy-start.5
  3.9 0.6 copy-start.6
  3.9 23.6 %collective-permute-start.4 = (bf16[576,3072]{1,0:T(8,128)(2,1)}, bf16[576,3072]{1,0:T(8,128)(2,1)}, u32[]{:S(2)}, u32[]{:S(2)}) collective-permute-start(bf16[576,3072]{1,0:T(8,128)(2,1)} %bitcast.22), channel_id=1, source_target_pairs={{0,16},{16,0},{1,17},{17,1},{2,18},{18,2},{3,19},{19,3},{4,20},{20... | collective-permute-start | bytes 10616840 | tf_op jit(solution)/shard_map/ppermute | solution.py:416
  4.1 23.4 %collective-permute-start.5 = (bf16[192,3072]{1,0:T(8,128)(2,1)}, bf16[192,3072]{1,0:T(8,128)(2,1)S(1)}, u32[]{:S(2)}, u32[]{:S(2)}) collective-permute-start(bf16[192,3072]{1,0:T(8,128)(2,1)} %bitcast.25), channel_id=1, source_target_pairs={{0,16},{16,0},{1,17},{17,1},{2,18},{18,2},{3,19},{19,3},{4,20},{20... | collective-permute-start | bytes 3538952 | tf_op jit(solution)/shard_map/ppermute | solution.py:416
  27.5 6.8 %copy-start.1 = (bf16[1,3072,576]{1,2,0:T(8,128)(2,1)S(1)}, bf16[1,3072,576]{1,2,0:T(8,128)(2,1)}, u32[]{:S(2)}) copy-start(bf16[1,3072,576]{1,2,0:T(8,128)(2,1)} %param.10) | copy-start | bytes 10616836
  31.3 5.4 %collective-permute-start.6 = (bf16[72,128]{1,0:T(8,128)(2,1)S(1)}, bf16[72,128]{1,0:T(8,128)(2,1)S(1)}, u32[]{:S(2)}, u32[]{:S(2)}) collective-permute-start(bf16[72,128]{1,0:T(8,128)(2,1)S(1)} %get-tuple-element.32), channel_id=1, source_target_pairs={{0,11},{1,12},{2,13},{3,14},{4,15},{5,0},{6,1},{7,2},{8,3},{9,4},{... | collective-permute-start | bytes 55304 | tf_op jit(solution)/shard_map/ppermute | solution.py:422
  32.2 5.6 %copy-start.3 = (s32[1,2,16]{2,1,0:T(2,128)S(1)}, s32[1,2,16]{2,1,0:T(2,128)}, u32[]{:S(2)}) copy-start(s32[1,2,16]{2,1,0:T(2,128)} %fresh.3) | copy-start | bytes 388
  32.2 5.6 %copy-start.4 = (s32[2,16]{1,0:T(2,128)S(1)}, s32[2,16]{1,0:T(2,128)}, u32[]{:S(2)}) copy-start(s32[2,16]{1,0:T(2,128)} %live.3) | copy-start | bytes 388
  32.2 23.2 %copy-start.2 = (bf16[1,3072,192]{1,2,0:T(8,128)(2,1)S(1)}, bf16[1,3072,192]{1,2,0:T(8,128)(2,1)}, u32[]{:S(2)}) copy-start(bf16[1,3072,192]{1,2,0:T(8,128)(2,1)} %param.11) | copy-start | bytes 3538948
  32.2 5.6 %collective-permute-start.7 = (bf16[72,128]{1,0:T(8,128)(2,1)S(1)}, bf16[72,128]{1,0:T(8,128)(2,1)S(1)}, u32[]{:S(2)}, u32[]{:S(2)}) collective-permute-start(bf16[72,128]{1,0:T(8,128)(2,1)S(1)} %get-tuple-element.33), channel_id=1, source_target_pairs={{0,6},{1,7},{2,8},{3,9},{4,10},{5,11},{6,12},{7,13},{8,14},{9,15},... | collective-permute-start | bytes 55304 | tf_op jit(solution)/shard_map/ppermute | solution.py:422
  71.4 4.7 %collective-permute-start.8 = (bf16[72,128]{1,0:T(8,128)(2,1)S(1)}, bf16[72,128]{1,0:T(8,128)(2,1)S(1)}, u32[]{:S(2)}, u32[]{:S(2)}) collective-permute-start(bf16[72,128]{1,0:T(8,128)(2,1)S(1)} %get-tuple-element.41), channel_id=1, source_target_pairs={{0,11},{1,12},{2,13},{3,14},{4,15},{5,0},{6,1},{7,2},{8,3},{9,4},{... | collective-permute-start | bytes 55304 | tf_op jit(solution)/shard_map/ppermute | solution.py:422
  72.2 5.6 %collective-permute-start.9 = (bf16[72,128]{1,0:T(8,128)(2,1)S(1)}, bf16[72,128]{1,0:T(8,128)(2,1)S(1)}, u32[]{:S(2)}, u32[]{:S(2)}) collective-permute-start(bf16[72,128]{1,0:T(8,128)(2,1)S(1)} %get-tuple-element.42), channel_id=1, source_target_pairs={{0,6},{1,7},{2,8},{3,9},{4,10},{5,11},{6,12},{7,13},{8,14},{9,15},... | collective-permute-start | bytes 55304 | tf_op jit(solution)/shard_map/ppermute | solution.py:422

commit v3 on v1

--- a/solution.py
+++ b/solution.py
@@ -425,6 +425,9 @@
     old_keys = jnp.transpose(k_stale[0], (1, 0, 2))
     old_values = jnp.transpose(v_stale[0], (1, 0, 2))
 
+    other_keys, sent_out = lax.optimization_barrier((swap_sections(old_keys), own_out))
+    other_out = swap_sections(sent_out)
+    out = (own_out, other_out)
     leaving = call(
         first_exchange,
         shape((n, 4, width), BF16),
@@ -433,18 +436,17 @@
         jnp.transpose(hidden, (1, 0, 2)),
         old_keys,
         old_values,
-        swap_sections(old_keys),
+        other_keys,
         swap_sections(old_values),
         specs=[HBM] * 3 + [ANY] * 2,
         spare=4 << 20,
     )
-    leaving, other_mod, other_fresh, sent_qkv, sent_out = lax.optimization_barrier(
-        (leaving, swap_sections(mod), swap_sections(fresh), own_qkv, own_out)
+    leaving, other_mod, other_fresh, sent_qkv = lax.optimization_barrier(
+        (leaving, swap_sections(mod), swap_sections(fresh), own_qkv)
     )
     mods = (mod, other_mod)
     flags = (fresh, other_fresh)
-    other_qkv, other_out = swap_sections(sent_qkv), swap_sections(sent_out)
-    out = (own_out, other_out)
+    other_qkv = swap_sections(sent_qkv)
     held_qkv = lax.ppermute(sent_qkv, "section", [(0, 0)])
     arrived = exchange(leaving, "blk")
 

time: 100 us -> 100 us (level)
  no operation moved by 1% of the time
where the time goes in v3:
time: 100 us; the launch traced here: 99.7 us
  blocking collectives  70 us (70%)
  starting transfers between devices  11 us (11%)
  Pallas kernels  10.3 us (10%)
  waiting for transfers between devices  6.6 us (7%)
    all_to_all x5, blocking collectives, exchange(): return lax.all_to_all(blocks, axis, split_axis=0, concat_axis=0, tiled=True)  70 us
    pallas_call x9, Pallas kernels, call(): pl.pallas_call(body, out_shape=outs, in_specs=specs or [VMEM] * len(args)...  10.3 us
    ppermute x4, starting transfers between devices, by_heads(): lax.ppermute(chunk, 'blk', [(b, (b + inverse * j) % n) for b in range(n)])  6.82 us
    ppermute x4, waiting for transfers between devices, by_heads(): lax.ppermute(chunk, 'blk', [(b, (b + inverse * j) % n) for b in range(n)])  6.58 us
    ppermute x1, starting transfers between devices, per_device(): held_qkv = lax.ppermute(sent_qkv, 'section', [(0, 0)])  2.64 us
  transfers between devices with their start and end apart: 11, of which 4 were waited for; matrix products, arithmetic and copies ran while one was open for 0% of the time, Pallas kernels for 2%

profile of v3, /device:TPU:0, one launch (start us, length us, event | category | flops | bytes accessed | tf_op | source)
XLA Modules:
  0.0 99.7 jit_solution(1081305824246032768)
XLA Ops:
  0.0 0.0 copy-start
  0.0 0.5 collective-permute-start
  0.5 0.1 collective-permute-start.1
  1.2 0.3 copy-done
  1.5 0.5 collective-permute-start.2
  2.0 0.1 collective-permute-start.3
  2.0 0.0 collective-permute-done.other_keys
  2.0 0.0 copy-start.5
  2.0 0.0 collective-permute-done.1.other_values
  2.0 0.0 copy-start.6
  2.0 0.6 copy-done.5
  2.6 0.0 copy-done.6
  2.6 1.9 %shard_map.91 = bf16[16,4,3072]{2,1,0:T(4,128)(2,1)} custom-call(bf16[3,2,3072]{2,1,0:T(2,128)(2,1)} %bitcast.28, bf16[3,2,3072]{2,1,0:T(2,128)(2,1)} %bitcast.30, bf16[3,2,3072]{2,1,0:T(2,128)(2,1)} %bitcast.32, bf16[3,2,3072]{2,1,0:T(2,128)(2,1)} %copy-done.5, bf16[3,2,3072]{2,1,0:T(2,128)(2,1)} %copy-done.6), custom_call_target="tpu_custom_call" | custom-call | bytes 1000000 | tf_op jit(solution)/shard_map/pallas_call | solution.py:135
  4.5 0.0 collective-permute-done.3.other_fresh
  4.5 0.0 collective-permute-done.2.other_mod
  4.6 0.5 collective-permute-start.5
  5.1 2.6 %collective-permute-start.4 = (bf16[576,3072]{1,0:T(8,128)(2,1)}, bf16[576,3072]{1,0:T(8,128)(2,1)S(1)}, u32[]{:S(2)}, u32[]{:S(2)}) collective-permute-start(bf16[576,3072]{1,0:T(8,128)(2,1)} %bitcast.26), channel_id=1, source_target_pairs={{0,0},{1,1},{2,2},{3,3},{4,4},{5,5},{6,6},{7,7},{8,8},{9,9},{10,10... | collective-permute-start | bytes 10616840 | tf_op jit(solution)/shard_map/ppermute | solution.py:450
  7.7 0.0 collective-permute-start.6
  7.7 21.1 %all_to_all.25.arrived = bf16[16,4,3072]{2,1,0:T(4,128)(2,1)S(1)} all-to-all(bf16[16,4,3072]{2,1,0:T(4,128)(2,1)} %shard_map.91), channel_id=1, replica_groups=mesh['section'=2,'blk'=16] {'blk'}, dimensions={0} | all-to-all | bytes 786432 | tf_op jit(solution)/shard_map/all_to_all | solution.py:387
  28.8 0.0 copy-start.3
  28.8 0.0 collective-permute-done.6.other_out.other
  28.8 0.0 collective-permute-done.5.other
  28.8 0.0 collective-permute-done.4.own
  28.8 1.7 %shard_map.92 = (bf16[72,128]{1,0:T(8,128)(2,1)S(1)}, bf16[72,128]{1,0:T(8,128)(2,1)S(1)}, bf16[72,128]{1,0:T(8,128)(2,1)S(1)}, bf16[48,192]{1,0:T(8,128)(2,1)S(1)}) custom-call(bf16[16,4,3072]{2,1,0:T(4,128)(2,1)S(1)} %all_to_all.25.arrived, bf16[576,3072]{1,0:T(8,128)(2,1)S(1)} %collective-permute-done.4.own, ...), custom_call_target="tpu_custom_call" | custom-call | flops 169869312 | bytes 4718592 | tf_op jit(solution)/shard_map/pallas_call | solution.py:135
  30.5 0.9 collective-permute-start.7
  31.5 2.0 %collective-permute-start.8 = (bf16[72,128]{1,0:T(8,128)(2,1)S(1)}, bf16[72,128]{1,0:T(8,128)(2,1)S(1)}, u32[]{:S(2)}, u32[]{:S(2)}) collective-permute-start(bf16[72,128]{1,0:T(8,128)(2,1)S(1)} %get-tuple-element.31), channel_id=1, source_target_pairs={{0,6},{1,7},{2,8},{3,9},{4,10},{5,11},{6,12},{7,13},{8,14},{9,15},... | collective-permute-start | bytes 55304 | tf_op jit(solution)/shard_map/ppermute | solution.py:397
  33.5 0.1 shard_map.93.old
  33.6 1.6 %collective-permute-done.7.chunk1 = bf16[72,128]{1,0:T(8,128)(2,1)S(1)} collective-permute-done((bf16[72,128]{1,0:T(8,128)(2,1)S(1)}, bf16[72,128]{1,0:T(8,128)(2,1)S(1)}, u32[]{:S(2)}, u32[]{:S(2)}) %collective-permute-start.7) | collective-permute-done | bytes 18464 | tf_op jit(solution)/shard_map/ppermute | solution.py:397
  35.2 1.8 %collective-permute-done.8.chunk2 = bf16[72,128]{1,0:T(8,128)(2,1)S(1)} collective-permute-done((bf16[72,128]{1,0:T(8,128)(2,1)S(1)}, bf16[72,128]{1,0:T(8,128)(2,1)S(1)}, u32[]{:S(2)}, u32[]{:S(2)}) %collective-permute-start.8) | collective-permute-done | bytes 18464 | tf_op jit(solution)/shard_map/ppermute | solution.py:397
  37.0 0.0 copy-done.3
  37.0 0.0 copy-done.4
  37.0 1.3 %shard_map.94 = bf16[16,72,128]{2,1,0:T(8,128)(2,1)S(1)} custom-call(bf16[72,128]{1,0:T(8,128)(2,1)S(1)} %get-tuple-element.28.chunk0, bf16[72,128]{1,0:T(8,128)(2,1)S(1)} %collective-permute-done.7.chunk1, bf16[72,128]{1,0:T(8,128)(2,1)S(1)} %collective-permute-done.8.chunk2, bf16[2,48,384]{2,1,0:T(8,128)(2,1)S(1)} %shard_map.93.old, ...), custom_call_target="tpu_custom_call" | custom-call | flops 3538944 | bytes 300000 | tf_op jit(solution)/shard_map/pallas_call | solution.py:135
  38.3 0.0 copy-start.2
  38.3 14.0 %all_to_all.26.blocks = bf16[16,72,128]{2,1,0:T(8,128)(2,1)S(1)} all-to-all(bf16[16,72,128]{2,1,0:T(8,128)(2,1)S(1)} %shard_map.94), channel_id=1, replica_groups=mesh['section'=2,'blk'=16] {'blk'}, dimensions={0} | all-to-all | bytes 589824 | tf_op jit(solution)/shard_map/all_to_all | solution.py:387
  52.3 0.0 copy-done.1
  52.3 0.9 shard_map.95
  53.2 12.2 %all_to_all.27.blocks = bf16[16,72,128]{2,1,0:T(8,128)(2,1)S(1)} all-to-all(bf16[16,72,128]{2,1,0:T(8,128)(2,1)S(1)} %get-tuple-element.35), channel_id=1, replica_groups=mesh['section'=2,'blk'=16] {'blk'}, dimensions={0} | all-to-all | bytes 589824 | tf_op jit(solution)/shard_map/all_to_all | solution.py:387
  65.4 0.0 copy-done.2
  65.4 1.7 %shard_map.96 = (bf16[72,128]{1,0:T(8,128)(2,1)S(1)}, bf16[72,128]{1,0:T(8,128)(2,1)S(1)}, bf16[72,128]{1,0:T(8,128)(2,1)S(1)}, bf16[48,192]{1,0:T(8,128)(2,1)S(1)}) custom-call(bf16[16,72,128]{2,1,0:T(8,128)(2,1)S(1)} %all_to_all.27.blocks, bf16[576,3072]{1,0:T(8,128)(2,1)S(1)} %bitcast.27, bf16[576,3072]{1,0:T(8,128)(2,1)S(1)} %collective-permute-done.5.other, ...), custom_call_target="tpu_custom_call" | custom-call | flops 169869312 | bytes 4718592 | tf_op jit(solution)/shard_map/pallas_call | solution.py:135
  67.1 1.5 %collective-permute-start.9 = (bf16[72,128]{1,0:T(8,128)(2,1)S(1)}, bf16[72,128]{1,0:T(8,128)(2,1)S(1)}, u32[]{:S(2)}, u32[]{:S(2)}) collective-permute-start(bf16[72,128]{1,0:T(8,128)(2,1)S(1)} %get-tuple-element.37), channel_id=1, source_target_pairs={{0,11},{1,12},{2,13},{3,14},{4,15},{5,0},{6,1},{7,2},{8,3},{9,4},{... | collective-permute-start | bytes 55304 | tf_op jit(solution)/shard_map/ppermute | solution.py:397
  68.5 2.4 %collective-permute-start.10 = (bf16[72,128]{1,0:T(8,128)(2,1)S(1)}, bf16[72,128]{1,0:T(8,128)(2,1)S(1)}, u32[]{:S(2)}, u32[]{:S(2)}) collective-permute-start(bf16[72,128]{1,0:T(8,128)(2,1)S(1)} %get-tuple-element.38), channel_id=1, source_target_pairs={{0,6},{1,7},{2,8},{3,9},{4,10},{5,11},{6,12},{7,13},{8,14},{9,15},... | collective-permute-start | bytes 55304 | tf_op jit(solution)/shard_map/ppermute | solution.py:397
  71.0 0.8 collective-permute-done.9.chunk1
  71.7 2.4 %collective-permute-done.10.chunk2 = bf16[72,128]{1,0:T(8,128)(2,1)S(1)} collective-permute-done((bf16[72,128]{1,0:T(8,128)(2,1)S(1)}, bf16[72,128]{1,0:T(8,128)(2,1)S(1)}, u32[]{:S(2)}, u32[]{:S(2)}) %collective-permute-start.10) | collective-permute-done | bytes 18464 | tf_op jit(solution)/shard_map/ppermute | solution.py:397
  74.1 1.3 %shard_map.97 = bf16[16,72,128]{2,1,0:T(8,128)(2,1)S(1)} custom-call(bf16[72,128]{1,0:T(8,128)(2,1)S(1)} %get-tuple-element.36.chunk0, bf16[72,128]{1,0:T(8,128)(2,1)S(1)} %collective-permute-done.9.chunk1, bf16[72,128]{1,0:T(8,128)(2,1)S(1)} %collective-permute-done.10.chunk2, bf16[2,48,384]{2,1,0:T(8,128)(2,1)S(1)} %shard_map.93.old, ...), custom_call_target="tpu_custom_call" | custom-call | flops 3538944 | bytes 300000 | tf_op jit(solution)/shard_map/pallas_call | solution.py:135
  75.4 13.1 %all_to_all.28.blocks = bf16[16,72,128]{2,1,0:T(8,128)(2,1)S(1)} all-to-all(bf16[16,72,128]{2,1,0:T(8,128)(2,1)S(1)} %shard_map.97), channel_id=1, replica_groups=mesh['section'=2,'blk'=16] {'blk'}, dimensions={0} | all-to-all | bytes 589824 | tf_op jit(solution)/shard_map/all_to_all | solution.py:387
  88.5 0.7 shard_map.98
  89.2 9.7 %all_to_all.29.arrived = bf16[32,4,192]{2,1,0:T(4,128)(2,1)S(1)} all-to-all(bf16[32,4,192]{2,1,0:T(4,128)(2,1)S(1)} %shard_map.98), channel_id=1, replica_groups=mesh['section'=2,'blk'=16] {'section','blk'}, dimensions={0} | all-to-all | bytes 98304 | tf_op jit(solution)/shard_map/all_to_all | solution.py:387
  98.9 0.8 shard_map.99
  (3 shorter events, 0.0 us)
Async XLA Ops:
  0.0 1.5 %copy-start = (f32[1,50,3,3072]{3,0,2,1:T(1,128)S(1)}, f32[1,50,3,3072]{3,0,2,1:T(1,128)}, u32[]{:S(2)}) copy-start(f32[1,50,3,3072]{3,0,2,1:T(1,128)} %param.12) | copy-start | bytes 5529604
  0.0 2.0 %collective-permute-start = (bf16[3,2,3072]{2,1,0:T(2,128)(2,1)}, bf16[3,2,3072]{2,1,0:T(2,128)(2,1)S(1)}, u32[]{:S(2)}, u32[]{:S(2)}) collective-permute-start(bf16[3,2,3072]{2,1,0:T(2,128)(2,1)} %bitcast.29), channel_id=1, source_target_pairs={{0,16},{16,0},{1,17},{17,1},{2,18},{18,2},{3,19},{19,3},{4,20},{20... | collective-permute-start | bytes 110600 | tf_op jit(solution)/shard_map/ppermute | solution.py:391
  0.5 1.6 %collective-permute-start.1 = (bf16[3,2,3072]{2,1,0:T(2,128)(2,1)}, bf16[3,2,3072]{2,1,0:T(2,128)(2,1)S(1)}, u32[]{:S(2)}, u32[]{:S(2)}) collective-permute-start(bf16[3,2,3072]{2,1,0:T(2,128)(2,1)} %bitcast.31), channel_id=1, source_target_pairs={{0,16},{16,0},{1,17},{17,1},{2,18},{18,2},{3,19},{19,3},{4,20},{20... | collective-permute-start | bytes 110600 | tf_op jit(solution)/shard_map/ppermute | solution.py:391
  1.5 3.0 %collective-permute-start.2 = (f32[3,1,3072]{2,1,0:T(1,128)S(1)}, f32[3,1,3072]{2,1,0:T(1,128)S(1)}, u32[]{:S(2)}, u32[]{:S(2)}) collective-permute-start(f32[3,1,3072]{2,1,0:T(1,128)S(1)} %dynamic-slice_bitcast_fusion.mod), channel_id=1, source_target_pairs={{0,16},{16,0},{1,17},{17,1},{2,18},{18,2},{3,19},{19,3},{4,20},{20... | collective-permute-start | bytes 110600 | tf_op jit(solution)/shard_map/ppermute | solution.py:391
  2.0 2.6 %collective-permute-start.3 = (s32[1,2,16]{2,1,0:T(2,128)}, s32[1,2,16]{2,1,0:T(2,128)S(1)}, u32[]{:S(2)}, u32[]{:S(2)}) collective-permute-start(s32[1,2,16]{2,1,0:T(2,128)} %fresh.3), channel_id=1, source_target_pairs={{0,16},{16,0},{1,17},{17,1},{2,18},{18,2},{3,19},{19,3},{4,20},{20... | collective-permute-start | bytes 392 | tf_op jit(solution)/shard_map/ppermute | solution.py:391
  2.0 0.6 copy-start.5
  2.0 0.6 copy-start.6
  4.6 24.2 %collective-permute-start.5 = (bf16[576,3072]{1,0:T(8,128)(2,1)}, bf16[576,3072]{1,0:T(8,128)(2,1)S(1)}, u32[]{:S(2)}, u32[]{:S(2)}) collective-permute-start(bf16[576,3072]{1,0:T(8,128)(2,1)} %bitcast.25), channel_id=1, source_target_pairs={{0,16},{16,0},{1,17},{17,1},{2,18},{18,2},{3,19},{19,3},{4,20},{20... | collective-permute-start | bytes 10616840 | tf_op jit(solution)/shard_map/ppermute | solution.py:391
  5.1 23.7 %collective-permute-start.4 = (bf16[576,3072]{1,0:T(8,128)(2,1)}, bf16[576,3072]{1,0:T(8,128)(2,1)S(1)}, u32[]{:S(2)}, u32[]{:S(2)}) collective-permute-start(bf16[576,3072]{1,0:T(8,128)(2,1)} %bitcast.26), channel_id=1, source_target_pairs={{0,0},{1,1},{2,2},{3,3},{4,4},{5,5},{6,6},{7,7},{8,8},{9,9},{10,10... | collective-permute-start | bytes 10616840 | tf_op jit(solution)/shard_map/ppermute | solution.py:450
  7.7 21.1 %collective-permute-start.6 = (bf16[192,3072]{1,0:T(8,128)(2,1)}, bf16[192,3072]{1,0:T(8,128)(2,1)S(1)}, u32[]{:S(2)}, u32[]{:S(2)}) collective-permute-start(bf16[192,3072]{1,0:T(8,128)(2,1)} %bitcast.22), channel_id=1, source_target_pairs={{0,16},{16,0},{1,17},{17,1},{2,18},{18,2},{3,19},{19,3},{4,20},{20... | collective-permute-start | bytes 3538952 | tf_op jit(solution)/shard_map/ppermute | solution.py:391
  28.8 8.3 %copy-start.3 = (s32[1,2,16]{2,1,0:T(2,128)S(1)}, s32[1,2,16]{2,1,0:T(2,128)}, u32[]{:S(2)}) copy-start(s32[1,2,16]{2,1,0:T(2,128)} %fresh.3) | copy-start | bytes 388
  28.8 8.3 %copy-start.4 = (s32[2,16]{1,0:T(2,128)S(1)}, s32[2,16]{1,0:T(2,128)}, u32[]{:S(2)}) copy-start(s32[2,16]{1,0:T(2,128)} %live.3) | copy-start | bytes 388
  30.5 21.8 %copy-start.1 = (bf16[1,3072,192]{1,2,0:T(8,128)(2,1)S(1)}, bf16[1,3072,192]{1,2,0:T(8,128)(2,1)}, u32[]{:S(2)}) copy-start(bf16[1,3072,192]{1,2,0:T(8,128)(2,1)} %param.11) | copy-start | bytes 3538948
  30.5 4.7 %collective-permute-start.7 = (bf16[72,128]{1,0:T(8,128)(2,1)S(1)}, bf16[72,128]{1,0:T(8,128)(2,1)S(1)}, u32[]{:S(2)}, u32[]{:S(2)}) collective-permute-start(bf16[72,128]{1,0:T(8,128)(2,1)S(1)} %get-tuple-element.30), channel_id=1, source_target_pairs={{0,11},{1,12},{2,13},{3,14},{4,15},{5,0},{6,1},{7,2},{8,3},{9,4},{... | collective-permute-start | bytes 55304 | tf_op jit(solution)/shard_map/ppermute | solution.py:397
  31.5 5.6 %collective-permute-start.8 = (bf16[72,128]{1,0:T(8,128)(2,1)S(1)}, bf16[72,128]{1,0:T(8,128)(2,1)S(1)}, u32[]{:S(2)}, u32[]{:S(2)}) collective-permute-start(bf16[72,128]{1,0:T(8,128)(2,1)S(1)} %get-tuple-element.31), channel_id=1, source_target_pairs={{0,6},{1,7},{2,8},{3,9},{4,10},{5,11},{6,12},{7,13},{8,14},{9,15},... | collective-permute-start | bytes 55304 | tf_op jit(solution)/shard_map/ppermute | solution.py:397
  38.3 27.0 %copy-start.2 = (bf16[1,3072,576]{1,2,0:T(8,128)(2,1)S(1)}, bf16[1,3072,576]{1,2,0:T(8,128)(2,1)}, u32[]{:S(2)}) copy-start(bf16[1,3072,576]{1,2,0:T(8,128)(2,1)} %param.10) | copy-start | bytes 10616836
  67.1 4.7 %collective-permute-start.9 = (bf16[72,128]{1,0:T(8,128)(2,1)S(1)}, bf16[72,128]{1,0:T(8,128)(2,1)S(1)}, u32[]{:S(2)}, u32[]{:S(2)}) collective-permute-start(bf16[72,128]{1,0:T(8,128)(2,1)S(1)} %get-tuple-element.37), channel_id=1, source_target_pairs={{0,11},{1,12},{2,13},{3,14},{4,15},{5,0},{6,1},{7,2},{8,3},{9,4},{... | collective-permute-start | bytes 55304 | tf_op jit(solution)/shard_map/ppermute | solution.py:397
  68.5 5.6 %collective-permute-start.10 = (bf16[72,128]{1,0:T(8,128)(2,1)S(1)}, bf16[72,128]{1,0:T(8,128)(2,1)S(1)}, u32[]{:S(2)}, u32[]{:S(2)}) collective-permute-start(bf16[72,128]{1,0:T(8,128)(2,1)S(1)} %get-tuple-element.38), channel_id=1, source_target_pairs={{0,6},{1,7},{2,8},{3,9},{4,10},{5,11},{6,12},{7,13},{8,14},{9,15},... | collective-permute-start | bytes 55304 | tf_op jit(solution)/shard_map/ppermute | solution.py:397

commit v4 on v3

--- a/solution.py
+++ b/solution.py
@@ -143,6 +143,10 @@
     )(*args)
 
 
+def pinned(array):
+    return pltpu.with_memory_space_constraint(array, pltpu.HBM)
+
+
 def dot_nt(left, right):
     return lax.dot_general(left, right, NT, preferred_element_type=F32)
 
@@ -240,13 +244,32 @@
         chunk[...] = pack(columns[:, 192 * j : 192 * j + 192])
 
 
-def first_projection(arrived, own, other, mod, other_mod, other_out, chunk0, chunk1, chunk2, residual, stream, scales, normed, columns):
+def first_projection(arrived, own, other, mod, other_mod, other_out, chunk0, chunk1, chunk2, residual, stream, scales, normed, columns, held, sems):
+    holds = lax.axis_index("section") == 0
+    parts = sems.shape[0]
+    size = held.shape[0] // parts
+    copies = [
+        pltpu.make_async_copy(own.at[pl.ds(i * size, size)], held.at[pl.ds(i * size, size)], sems.at[i])
+        for i in range(parts)
+    ]
+
+    @pl.when(holds)
+    def _():
+        for copy in copies:
+            copy.start()
+
     n = arrived.shape[0]
     rows = stream.shape[0] // n
     for b in range(n):
         stream[rows * b : rows * b + rows, :] = arrived[b, :rows, :].astype(F32)
     normalise(0, stream, mod, other_mod, normed, residual, scales)
-    dot_into(0, normed, own, other, columns)
+
+    @pl.when(holds)
+    def _():
+        for copy in copies:
+            copy.wait()
+
+    dot_into(0, normed, held, other, columns)
     chunks_of(columns, (chunk0, chunk1, chunk2))
 
 
@@ -425,29 +448,24 @@
     old_keys = jnp.transpose(k_stale[0], (1, 0, 2))
     old_values = jnp.transpose(v_stale[0], (1, 0, 2))
 
-    other_keys, sent_out = lax.optimization_barrier((swap_sections(old_keys), own_out))
-    other_out = swap_sections(sent_out)
+    small = [swap_sections(array) for array in (old_keys, old_values, mod, fresh)]
+    (other_keys, other_values, other_mod, other_fresh), sent_qkv, sent_out = lax.optimization_barrier(
+        (small, own_qkv, own_out)
+    )
+    mods = (mod, other_mod)
+    flags = (fresh, other_fresh)
+    other_qkv, other_out = swap_sections(sent_qkv), swap_sections(sent_out)
     out = (own_out, other_out)
     leaving = call(
         first_exchange,
         shape((n, 4, width), BF16),
         [pltpu.VMEM((5, rows, reqs, width), BF16), pltpu.SemaphoreType.DMA((5,))],
         (0, 1000000),
-        jnp.transpose(hidden, (1, 0, 2)),
-        old_keys,
-        old_values,
+        *(pinned(array) for array in (jnp.transpose(hidden, (1, 0, 2)), old_keys, old_values)),
         other_keys,
-        swap_sections(old_values),
+        other_values,
         specs=[HBM] * 3 + [ANY] * 2,
-        spare=4 << 20,
-    )
-    leaving, other_mod, other_fresh, sent_qkv = lax.optimization_barrier(
-        (leaving, swap_sections(mod), swap_sections(fresh), own_qkv)
-    )
-    mods = (mod, other_mod)
-    flags = (fresh, other_fresh)
-    other_qkv = swap_sections(sent_qkv)
-    held_qkv = lax.ppermute(sent_qkv, "section", [(0, 0)])
+    )
     arrived = exchange(leaving, "blk")
 
     blocks = arrived
@@ -460,11 +478,12 @@
                 pltpu.VMEM(mod.shape, F32),
                 pltpu.VMEM((tokens, width), BF16),
                 pltpu.VMEM((tokens, 3 * columns), BF16),
-            ],
+            ]
+            + ([] if layer else [pltpu.VMEM(own_qkv.shape, BF16), pltpu.SemaphoreType.DMA((36,))]),
             (2 * tokens * width * 3 * columns, 8 * width * columns),
             blocks,
-            *((own_qkv, other_qkv, *mods) if layer else (held_qkv, other_qkv, *mods, other_out)),
-            **({} if layer else {"specs": [VMEM] * 5 + [ANY]}),
+            *((own_qkv, other_qkv, *mods) if layer else (pinned(own_qkv), other_qkv, *mods, other_out)),
+            **({} if layer else {"specs": [VMEM, HBM, VMEM, VMEM, VMEM, ANY]}),
         )
         if layer == 0:
             arrived, chunks[1] = lax.optimization_barrier((arrived, chunks[1]))

time: 100 us -> 99.7 us (level)
  starting transfers between devices: 11 us -> 8.38 us
  Pallas kernels: 10.3 us -> 11.5 us
  waiting for transfers between devices: 6.6 us -> 7.65 us
    ppermute x1 -> x0, starting transfers between devices: 2.64 us -> none  [per_device(): held_qkv = lax.ppermute(sent_qkv, 'section', [(0, 0)])]
    ppermute x6, waiting for transfers between devices: 0.02 us -> 1.31 us  [swap_sections(): return lax.ppermute(array, 'section', [(0, 1), (1, 0)])]
    pallas_call x9, Pallas kernels: 10.3 us -> 11.5 us  [call(): pl.pallas_call(body, out_shape=outs, in_specs=specs or [VMEM] * len(args)...]
  transfers between devices with their start and end apart: 11 -> 10, of which waited for: 4 -> 5; matrix products, arithmetic and copies ran while one was open for 0% -> 0% of each run, Pallas kernels for 2% -> 1%
where the time goes in v4:
time: 99.7 us; the launch traced here: 99.4 us
  blocking collectives  70.2 us (70%)
  Pallas kernels  11.5 us (12%)
  starting transfers between devices  8.38 us (8%)
  waiting for transfers between devices  7.65 us (8%)
    all_to_all x5, blocking collectives, exchange(): return lax.all_to_all(blocks, axis, split_axis=0, concat_axis=0, tiled=True)  70.2 us
    pallas_call x9, Pallas kernels, call(): pl.pallas_call(body, out_shape=outs, in_specs=specs or [VMEM] * len(args)...  11.5 us
    ppermute x4, starting transfers between devices, by_heads(): lax.ppermute(chunk, 'blk', [(b, (b + inverse * j) % n) for b in range(n)])  6.79 us
    ppermute x4, waiting for transfers between devices, by_heads(): lax.ppermute(chunk, 'blk', [(b, (b + inverse * j) % n) for b in range(n)])  6.34 us
  transfers between devices with their start and end apart: 10, of which 5 were waited for; matrix products, arithmetic and copies ran while one was open for 0% of the time, Pallas kernels for 1%

profile of v4, /device:TPU:0, one launch (start us, length us, event | category | flops | bytes accessed | tf_op | source)
XLA Modules:
  0.0 99.4 jit_solution(5977710535010970909)
XLA Ops:
  0.0 0.0 copy-start
  0.8 0.7 copy-done
  1.5 0.5 collective-permute-start.2
  2.0 0.1 collective-permute-start
  2.0 0.5 collective-permute-start.1
  2.5 0.1 collective-permute-start.3
  2.5 1.3 %collective-permute-done.3.other_fresh = s32[1,2,16]{2,1,0:T(2,128)S(1)} collective-permute-done((s32[1,2,16]{2,1,0:T(2,128)}, s32[1,2,16]{2,1,0:T(2,128)S(1)}, u32[]{:S(2)}, u32[]{:S(2)}) %collective-permute-start.3) | collective-permute-done | bytes 160 | tf_op jit(solution)/shard_map/ppermute | solution.py:414
  3.8 0.0 collective-permute-done.2.other_mod
  3.8 0.0 collective-permute-done.other_keys
  3.8 0.0 collective-permute-done.1.other_values
  3.9 0.3 collective-permute-start.4
  4.1 0.3 collective-permute-start.5
  4.4 1.1 %shard_map.91 = bf16[16,4,3072]{2,1,0:T(4,128)(2,1)S(1)} custom-call(bf16[3,2,3072]{2,1,0:T(2,128)(2,1)} %bitcast.28, bf16[3,2,3072]{2,1,0:T(2,128)(2,1)} %bitcast.30, bf16[3,2,3072]{2,1,0:T(2,128)(2,1)} %bitcast.32, bf16[3,2,3072]{2,1,0:T(2,128)(2,1)S(1)} %collective-permute-done.other_keys, bf16[3,2,3072]{2,1,0:T(2,128)(2,1)S(1)} %collective-permute-done.1.other_values), custom_call_target="tpu_custom_call" | custom-call | bytes 1000000 | tf_op jit(solution)/shard_map/pallas_call | solution.py:135
  5.5 20.9 %all_to_all.25.arrived = bf16[16,4,3072]{2,1,0:T(4,128)(2,1)S(1)} all-to-all(bf16[16,4,3072]{2,1,0:T(4,128)(2,1)S(1)} %shard_map.91), channel_id=1, replica_groups=mesh['section'=2,'blk'=16] {'blk'}, dimensions={0} | all-to-all | bytes 786432 | tf_op jit(solution)/shard_map/all_to_all | solution.py:410
  26.5 0.0 copy-start.3
  26.5 0.0 copy-start.4
  26.5 0.0 collective-permute-done.5.other_out.other
  26.5 0.0 collective-permute-done.4.other
  26.5 3.7 %shard_map.92 = (bf16[72,128]{1,0:T(8,128)(2,1)S(1)}, bf16[72,128]{1,0:T(8,128)(2,1)S(1)}, bf16[72,128]{1,0:T(8,128)(2,1)S(1)}, bf16[48,192]{1,0:T(8,128)(2,1)S(1)}) custom-call(bf16[16,4,3072]{2,1,0:T(4,128)(2,1)S(1)} %all_to_all.25.arrived, bf16[576,3072]{1,0:T(8,128)(2,1)} %bitcast.23, bf16[576,3072]{1,0:T(8,128)(2,1)S(1)} %collective-permute-done.4.other, ...), custom_call_target="tpu_custom_call" | custom-call | flops 169869312 | bytes 4718592 | tf_op jit(solution)/shard_map/pallas_call | solution.py:135
  30.2 0.0 copy-start.2
  30.2 0.9 collective-permute-start.6
  31.1 2.1 %collective-permute-start.7 = (bf16[72,128]{1,0:T(8,128)(2,1)S(1)}, bf16[72,128]{1,0:T(8,128)(2,1)S(1)}, u32[]{:S(2)}, u32[]{:S(2)}) collective-permute-start(bf16[72,128]{1,0:T(8,128)(2,1)S(1)} %get-tuple-element.31), channel_id=1, source_target_pairs={{0,6},{1,7},{2,8},{3,9},{4,10},{5,11},{6,12},{7,13},{8,14},{9,15},... | collective-permute-start | bytes 55304 | tf_op jit(solution)/shard_map/ppermute | solution.py:420
  33.2 0.1 shard_map.93.old
  33.3 1.6 %collective-permute-done.6.chunk1 = bf16[72,128]{1,0:T(8,128)(2,1)S(1)} collective-permute-done((bf16[72,128]{1,0:T(8,128)(2,1)S(1)}, bf16[72,128]{1,0:T(8,128)(2,1)S(1)}, u32[]{:S(2)}, u32[]{:S(2)}) %collective-permute-start.6) | collective-permute-done | bytes 18464 | tf_op jit(solution)/shard_map/ppermute | solution.py:420
  34.9 1.7 %collective-permute-done.7.chunk2 = bf16[72,128]{1,0:T(8,128)(2,1)S(1)} collective-permute-done((bf16[72,128]{1,0:T(8,128)(2,1)S(1)}, bf16[72,128]{1,0:T(8,128)(2,1)S(1)}, u32[]{:S(2)}, u32[]{:S(2)}) %collective-permute-start.7) | collective-permute-done | bytes 18464 | tf_op jit(solution)/shard_map/ppermute | solution.py:420
  36.6 0.0 copy-done.3
  36.6 0.0 copy-done.4
  36.6 1.3 %shard_map.94 = bf16[16,72,128]{2,1,0:T(8,128)(2,1)S(1)} custom-call(bf16[72,128]{1,0:T(8,128)(2,1)S(1)} %get-tuple-element.28.chunk0, bf16[72,128]{1,0:T(8,128)(2,1)S(1)} %collective-permute-done.6.chunk1, bf16[72,128]{1,0:T(8,128)(2,1)S(1)} %collective-permute-done.7.chunk2, bf16[2,48,384]{2,1,0:T(8,128)(2,1)S(1)} %shard_map.93.old, ...), custom_call_target="tpu_custom_call" | custom-call | flops 3538944 | bytes 300000 | tf_op jit(solution)/shard_map/pallas_call | solution.py:135
  38.0 0.0 copy-start.1
  38.0 14.0 %all_to_all.26.blocks = bf16[16,72,128]{2,1,0:T(8,128)(2,1)S(1)} all-to-all(bf16[16,72,128]{2,1,0:T(8,128)(2,1)S(1)} %shard_map.94), channel_id=1, replica_groups=mesh['section'=2,'blk'=16] {'blk'}, dimensions={0} | all-to-all | bytes 589824 | tf_op jit(solution)/shard_map/all_to_all | solution.py:410
  51.9 0.0 copy-done.2
  51.9 0.9 shard_map.95
  52.8 12.4 %all_to_all.27.blocks = bf16[16,72,128]{2,1,0:T(8,128)(2,1)S(1)} all-to-all(bf16[16,72,128]{2,1,0:T(8,128)(2,1)S(1)} %get-tuple-element.35), channel_id=1, replica_groups=mesh['section'=2,'blk'=16] {'blk'}, dimensions={0} | all-to-all | bytes 589824 | tf_op jit(solution)/shard_map/all_to_all | solution.py:410
  65.2 0.0 copy-done.1
  65.2 1.7 %shard_map.96 = (bf16[72,128]{1,0:T(8,128)(2,1)S(1)}, bf16[72,128]{1,0:T(8,128)(2,1)S(1)}, bf16[72,128]{1,0:T(8,128)(2,1)S(1)}, bf16[48,192]{1,0:T(8,128)(2,1)S(1)}) custom-call(bf16[16,72,128]{2,1,0:T(8,128)(2,1)S(1)} %all_to_all.27.blocks, bf16[576,3072]{1,0:T(8,128)(2,1)S(1)} %bitcast.24, bf16[576,3072]{1,0:T(8,128)(2,1)S(1)} %collective-permute-done.4.other, ...), custom_call_target="tpu_custom_call" | custom-call | flops 169869312 | bytes 4718592 | tf_op jit(solution)/shard_map/pallas_call | solution.py:135
  66.9 1.3 %collective-permute-start.8 = (bf16[72,128]{1,0:T(8,128)(2,1)S(1)}, bf16[72,128]{1,0:T(8,128)(2,1)S(1)}, u32[]{:S(2)}, u32[]{:S(2)}) collective-permute-start(bf16[72,128]{1,0:T(8,128)(2,1)S(1)} %get-tuple-element.37), channel_id=1, source_target_pairs={{0,11},{1,12},{2,13},{3,14},{4,15},{5,0},{6,1},{7,2},{8,3},{9,4},{... | collective-permute-start | bytes 55304 | tf_op jit(solution)/shard_map/ppermute | solution.py:420
  68.2 2.6 %collective-permute-start.9 = (bf16[72,128]{1,0:T(8,128)(2,1)S(1)}, bf16[72,128]{1,0:T(8,128)(2,1)S(1)}, u32[]{:S(2)}, u32[]{:S(2)}) collective-permute-start(bf16[72,128]{1,0:T(8,128)(2,1)S(1)} %get-tuple-element.38), channel_id=1, source_target_pairs={{0,6},{1,7},{2,8},{3,9},{4,10},{5,11},{6,12},{7,13},{8,14},{9,15},... | collective-permute-start | bytes 55304 | tf_op jit(solution)/shard_map/ppermute | solution.py:420
  70.7 0.9 collective-permute-done.8.chunk1
  71.6 2.2 %collective-permute-done.9.chunk2 = bf16[72,128]{1,0:T(8,128)(2,1)S(1)} collective-permute-done((bf16[72,128]{1,0:T(8,128)(2,1)S(1)}, bf16[72,128]{1,0:T(8,128)(2,1)S(1)}, u32[]{:S(2)}, u32[]{:S(2)}) %collective-permute-start.9) | collective-permute-done | bytes 18464 | tf_op jit(solution)/shard_map/ppermute | solution.py:420
  73.7 1.3 %shard_map.97 = bf16[16,72,128]{2,1,0:T(8,128)(2,1)S(1)} custom-call(bf16[72,128]{1,0:T(8,128)(2,1)S(1)} %get-tuple-element.36.chunk0, bf16[72,128]{1,0:T(8,128)(2,1)S(1)} %collective-permute-done.8.chunk1, bf16[72,128]{1,0:T(8,128)(2,1)S(1)} %collective-permute-done.9.chunk2, bf16[2,48,384]{2,1,0:T(8,128)(2,1)S(1)} %shard_map.93.old, ...), custom_call_target="tpu_custom_call" | custom-call | flops 3538944 | bytes 300000 | tf_op jit(solution)/shard_map/pallas_call | solution.py:135
  75.0 13.2 %all_to_all.28.blocks = bf16[16,72,128]{2,1,0:T(8,128)(2,1)S(1)} all-to-all(bf16[16,72,128]{2,1,0:T(8,128)(2,1)S(1)} %shard_map.97), channel_id=1, replica_groups=mesh['section'=2,'blk'=16] {'blk'}, dimensions={0} | all-to-all | bytes 589824 | tf_op jit(solution)/shard_map/all_to_all | solution.py:410
  88.2 0.7 shard_map.98
  88.9 9.7 %all_to_all.29.arrived = bf16[32,4,192]{2,1,0:T(4,128)(2,1)S(1)} all-to-all(bf16[32,4,192]{2,1,0:T(4,128)(2,1)S(1)} %shard_map.98), channel_id=1, replica_groups=mesh['section'=2,'blk'=16] {'section','blk'}, dimensions={0} | all-to-all | bytes 98304 | tf_op jit(solution)/shard_map/all_to_all | solution.py:410
  98.6 0.8 shard_map.99
  (1 shorter events, 0.0 us)
Async XLA Ops:
  0.0 1.5 %copy-start = (f32[1,50,3,3072]{3,0,2,1:T(1,128)S(1)}, f32[1,50,3,3072]{3,0,2,1:T(1,128)}, u32[]{:S(2)}) copy-start(f32[1,50,3,3072]{3,0,2,1:T(1,128)} %param.12) | copy-start | bytes 5529604
  1.5 2.3 %collective-permute-start.2 = (f32[3,1,3072]{2,1,0:T(1,128)S(1)}, f32[3,1,3072]{2,1,0:T(1,128)S(1)}, u32[]{:S(2)}, u32[]{:S(2)}) collective-permute-start(f32[3,1,3072]{2,1,0:T(1,128)S(1)} %dynamic-slice_bitcast_fusion.mod), channel_id=1, source_target_pairs={{0,16},{16,0},{1,17},{17,1},{2,18},{18,2},{3,19},{19,3},{4,20},{20... | collective-permute-start | bytes 110600 | tf_op jit(solution)/shard_map/ppermute | solution.py:414
  2.0 1.9 %collective-permute-start = (bf16[3,2,3072]{2,1,0:T(2,128)(2,1)}, bf16[3,2,3072]{2,1,0:T(2,128)(2,1)S(1)}, u32[]{:S(2)}, u32[]{:S(2)}) collective-permute-start(bf16[3,2,3072]{2,1,0:T(2,128)(2,1)} %bitcast.29), channel_id=1, source_target_pairs={{0,16},{16,0},{1,17},{17,1},{2,18},{18,2},{3,19},{19,3},{4,20},{20... | collective-permute-start | bytes 110600 | tf_op jit(solution)/shard_map/ppermute | solution.py:414
  2.0 1.8 %collective-permute-start.1 = (bf16[3,2,3072]{2,1,0:T(2,128)(2,1)}, bf16[3,2,3072]{2,1,0:T(2,128)(2,1)S(1)}, u32[]{:S(2)}, u32[]{:S(2)}) collective-permute-start(bf16[3,2,3072]{2,1,0:T(2,128)(2,1)} %bitcast.31), channel_id=1, source_target_pairs={{0,16},{16,0},{1,17},{17,1},{2,18},{18,2},{3,19},{19,3},{4,20},{20... | collective-permute-start | bytes 110600 | tf_op jit(solution)/shard_map/ppermute | solution.py:414
  2.5 1.4 %collective-permute-start.3 = (s32[1,2,16]{2,1,0:T(2,128)}, s32[1,2,16]{2,1,0:T(2,128)S(1)}, u32[]{:S(2)}, u32[]{:S(2)}) collective-permute-start(s32[1,2,16]{2,1,0:T(2,128)} %fresh.3), channel_id=1, source_target_pairs={{0,16},{16,0},{1,17},{17,1},{2,18},{18,2},{3,19},{19,3},{4,20},{20... | collective-permute-start | bytes 392 | tf_op jit(solution)/shard_map/ppermute | solution.py:414
  3.9 22.6 %collective-permute-start.4 = (bf16[576,3072]{1,0:T(8,128)(2,1)}, bf16[576,3072]{1,0:T(8,128)(2,1)S(1)}, u32[]{:S(2)}, u32[]{:S(2)}) collective-permute-start(bf16[576,3072]{1,0:T(8,128)(2,1)} %bitcast.22), channel_id=1, source_target_pairs={{0,16},{16,0},{1,17},{17,1},{2,18},{18,2},{3,19},{19,3},{4,20},{20... | collective-permute-start | bytes 10616840 | tf_op jit(solution)/shard_map/ppermute | solution.py:414
  4.1 22.4 %collective-permute-start.5 = (bf16[192,3072]{1,0:T(8,128)(2,1)}, bf16[192,3072]{1,0:T(8,128)(2,1)S(1)}, u32[]{:S(2)}, u32[]{:S(2)}) collective-permute-start(bf16[192,3072]{1,0:T(8,128)(2,1)} %bitcast.25), channel_id=1, source_target_pairs={{0,16},{16,0},{1,17},{17,1},{2,18},{18,2},{3,19},{19,3},{4,20},{20... | collective-permute-start | bytes 3538952 | tf_op jit(solution)/shard_map/ppermute | solution.py:414
  26.5 10.2 %copy-start.3 = (s32[1,2,16]{2,1,0:T(2,128)S(1)}, s32[1,2,16]{2,1,0:T(2,128)}, u32[]{:S(2)}) copy-start(s32[1,2,16]{2,1,0:T(2,128)} %fresh.3) | copy-start | bytes 388
  26.5 10.2 %copy-start.4 = (s32[2,16]{1,0:T(2,128)S(1)}, s32[2,16]{1,0:T(2,128)}, u32[]{:S(2)}) copy-start(s32[2,16]{1,0:T(2,128)} %live.3) | copy-start | bytes 388
  30.2 21.7 %copy-start.2 = (bf16[1,3072,192]{1,2,0:T(8,128)(2,1)S(1)}, bf16[1,3072,192]{1,2,0:T(8,128)(2,1)}, u32[]{:S(2)}) copy-start(bf16[1,3072,192]{1,2,0:T(8,128)(2,1)} %param.11) | copy-start | bytes 3538948
  30.2 4.7 %collective-permute-start.6 = (bf16[72,128]{1,0:T(8,128)(2,1)S(1)}, bf16[72,128]{1,0:T(8,128)(2,1)S(1)}, u32[]{:S(2)}, u32[]{:S(2)}) collective-permute-start(bf16[72,128]{1,0:T(8,128)(2,1)S(1)} %get-tuple-element.30), channel_id=1, source_target_pairs={{0,11},{1,12},{2,13},{3,14},{4,15},{5,0},{6,1},{7,2},{8,3},{9,4},{... | collective-permute-start | bytes 55304 | tf_op jit(solution)/shard_map/ppermute | solution.py:420
  31.1 5.6 %collective-permute-start.7 = (bf16[72,128]{1,0:T(8,128)(2,1)S(1)}, bf16[72,128]{1,0:T(8,128)(2,1)S(1)}, u32[]{:S(2)}, u32[]{:S(2)}) collective-permute-start(bf16[72,128]{1,0:T(8,128)(2,1)S(1)} %get-tuple-element.31), channel_id=1, source_target_pairs={{0,6},{1,7},{2,8},{3,9},{4,10},{5,11},{6,12},{7,13},{8,14},{9,15},... | collective-permute-start | bytes 55304 | tf_op jit(solution)/shard_map/ppermute | solution.py:420
  38.0 27.3 %copy-start.1 = (bf16[1,3072,576]{1,2,0:T(8,128)(2,1)S(1)}, bf16[1,3072,576]{1,2,0:T(8,128)(2,1)}, u32[]{:S(2)}) copy-start(bf16[1,3072,576]{1,2,0:T(8,128)(2,1)} %param.10) | copy-start | bytes 10616836
  66.9 4.7 %collective-permute-start.8 = (bf16[72,128]{1,0:T(8,128)(2,1)S(1)}, bf16[72,128]{1,0:T(8,128)(2,1)S(1)}, u32[]{:S(2)}, u32[]{:S(2)}) collective-permute-start(bf16[72,128]{1,0:T(8,128)(2,1)S(1)} %get-tuple-element.37), channel_id=1, source_target_pairs={{0,11},{1,12},{2,13},{3,14},{4,15},{5,0},{6,1},{7,2},{8,3},{9,4},{... | collective-permute-start | bytes 55304 | tf_op jit(solution)/shard_map/ppermute | solution.py:420
  68.2 5.6 %collective-permute-start.9 = (bf16[72,128]{1,0:T(8,128)(2,1)S(1)}, bf16[72,128]{1,0:T(8,128)(2,1)S(1)}, u32[]{:S(2)}, u32[]{:S(2)}) collective-permute-start(bf16[72,128]{1,0:T(8,128)(2,1)S(1)} %get-tuple-element.38), channel_id=1, source_target_pairs={{0,6},{1,7},{2,8},{3,9},{4,10},{5,11},{6,12},{7,13},{8,14},{9,15},... | collective-permute-start | bytes 55304 | tf_op jit(solution)/shard_map/ppermute | solution.py:420

commit v5 on v4

--- a/solution.py
+++ b/solution.py
@@ -244,32 +244,49 @@
         chunk[...] = pack(columns[:, 192 * j : 192 * j + 192])
 
 
-def first_projection(arrived, own, other, mod, other_mod, other_out, chunk0, chunk1, chunk2, residual, stream, scales, normed, columns, held, sems):
-    holds = lax.axis_index("section") == 0
+def fetch_if_held(layer, own, first_row, here, sems):
+    held = lax.axis_index("section") == layer
     parts = sems.shape[0]
-    size = held.shape[0] // parts
+    size = here.shape[0] // parts
     copies = [
-        pltpu.make_async_copy(own.at[pl.ds(i * size, size)], held.at[pl.ds(i * size, size)], sems.at[i])
+        pltpu.make_async_copy(own.at[pl.ds(first_row + i * size, size)], here.at[pl.ds(i * size, size)], sems.at[i])
         for i in range(parts)
     ]
 
-    @pl.when(holds)
+    @pl.when(held)
     def _():
         for copy in copies:
             copy.start()
 
+    def wait():
+        @pl.when(held)
+        def _():
+            for copy in copies:
+                copy.wait()
+
+    return wait
+
+
+def first_projection(arrived, early, own, other, mod, other_mod, other_out, chunk0, chunk1, chunk2, residual, stream, scales, normed, columns, late, sems):
+    wait = fetch_if_held(0, own, early.shape[0], late, sems)
     n = arrived.shape[0]
     rows = stream.shape[0] // n
     for b in range(n):
         stream[rows * b : rows * b + rows, :] = arrived[b, :rows, :].astype(F32)
     normalise(0, stream, mod, other_mod, normed, residual, scales)
+    wait()
+    holds = lax.axis_index("section") == 0
+    split = early.shape[0]
 
     @pl.when(holds)
     def _():
-        for copy in copies:
-            copy.wait()
-
-    dot_into(0, normed, held, other, columns)
+        columns[:, :split] = dot_nt(normed[...], early[...]).astype(BF16)
+        columns[:, split:] = dot_nt(normed[...], late[...]).astype(BF16)
+
+    @pl.when(jnp.logical_not(holds))
+    def _():
+        columns[...] = dot_nt(normed[...], other[...]).astype(BF16)
+
     chunks_of(columns, (chunk0, chunk1, chunk2))
 
 
@@ -353,13 +370,14 @@
             by_token[layer * n + b, :rows, :] = outs[rows * b : rows * b + rows, :].astype(BF16)
 
 
-def first_exchange(hidden, old_keys, old_values, other_keys, other_values, leaving, held, sems):
+def first_exchange(hidden, old_keys, old_values, other_keys, other_values, weight, leaving, early, held, sems, weight_sems):
     copies = [
         pltpu.make_async_copy(ref, held.at[i], sems.at[i])
         for i, ref in enumerate((hidden, old_keys, old_values, other_keys, other_values))
     ]
     for copy in copies:
         copy.start()
+    wait = fetch_if_held(0, weight, 0, early, weight_sems)
     rows, reqs, width = hidden.shape
     n = leaving.shape[0]
     columns = width // n
@@ -381,6 +399,7 @@
         leaving[b, :rows, :] = mine
         for i in range(rows):
             leaving[b, rows : rows + 1, i * 4 * columns : (i + 1) * 4 * columns] = block[i : i + 1].astype(BF16)
+    wait()
 
 
 def stale_by_token(arrived, old, rows):
@@ -456,15 +475,21 @@
     flags = (fresh, other_fresh)
     other_qkv, other_out = swap_sections(sent_qkv), swap_sections(sent_out)
     out = (own_out, other_out)
-    leaving = call(
+    split = 256
+    leaving, early = call(
         first_exchange,
-        shape((n, 4, width), BF16),
-        [pltpu.VMEM((5, rows, reqs, width), BF16), pltpu.SemaphoreType.DMA((5,))],
+        [shape((n, 4, width), BF16), shape((split, width), BF16)],
+        [
+            pltpu.VMEM((5, rows, reqs, width), BF16),
+            pltpu.SemaphoreType.DMA((5,)),
+            pltpu.SemaphoreType.DMA((16,)),
+        ],
         (0, 1000000),
         *(pinned(array) for array in (jnp.transpose(hidden, (1, 0, 2)), old_keys, old_values)),
         other_keys,
         other_values,
-        specs=[HBM] * 3 + [ANY] * 2,
+        pinned(own_qkv),
+        specs=[HBM] * 3 + [ANY] * 2 + [HBM],
     )
     arrived = exchange(leaving, "blk")
 
@@ -479,11 +504,11 @@
                 pltpu.VMEM((tokens, width), BF16),
                 pltpu.VMEM((tokens, 3 * columns), BF16),
             ]
-            + ([] if layer else [pltpu.VMEM(own_qkv.shape, BF16), pltpu.SemaphoreType.DMA((36,))]),
+            + ([] if layer else [pltpu.VMEM((3 * columns - split, width), BF16), pltpu.SemaphoreType.DMA((20,))]),
             (2 * tokens * width * 3 * columns, 8 * width * columns),
             blocks,
-            *((own_qkv, other_qkv, *mods) if layer else (pinned(own_qkv), other_qkv, *mods, other_out)),
-            **({} if layer else {"specs": [VMEM, HBM, VMEM, VMEM, VMEM, ANY]}),
+            *((own_qkv, other_qkv, *mods) if layer else (early, pinned(own_qkv), other_qkv, *mods, other_out)),
+            **({} if layer else {"specs": [VMEM, VMEM, HBM, VMEM, VMEM, VMEM, ANY]}),
         )
         if layer == 0:
             arrived, chunks[1] = lax.optimization_barrier((arrived, chunks[1]))

time: 99.7 us -> 99.6 us (level)
  transfers between devices with their start and end apart: 10 -> 10, of which waited for: 5 -> 5; matrix products, arithmetic and copies ran while one was open for 0% -> 0% of each run, Pallas kernels for 1% -> 2%
where the time goes in v5:
time: 99.6 us; the launch traced here: 99.2 us
  blocking collectives  69.8 us (70%)
  Pallas kernels  11.7 us (12%)
  starting transfers between devices  8.4 us (8%)
  waiting for transfers between devices  7.59 us (8%)
    all_to_all x5, blocking collectives, exchange(): return lax.all_to_all(blocks, axis, split_axis=0, concat_axis=0, tiled=True)  69.8 us
    pallas_call x9, Pallas kernels, call(): pl.pallas_call(body, out_shape=outs, in_specs=specs or [VMEM] * len(args)...  11.7 us
    ppermute x4, starting transfers between devices, by_heads(): lax.ppermute(chunk, 'blk', [(b, (b + inverse * j) % n) for b in range(n)])  6.81 us
    ppermute x4, waiting for transfers between devices, by_heads(): lax.ppermute(chunk, 'blk', [(b, (b + inverse * j) % n) for b in range(n)])  6.29 us
  transfers between devices with their start and end apart: 10, of which 5 were waited for; matrix products, arithmetic and copies ran while one was open for 0% of the time, Pallas kernels for 2%

profile of v5, /device:TPU:0, one launch (start us, length us, event | category | flops | bytes accessed | tf_op | source)
XLA Modules:
  0.0 99.2 jit_solution(4589239021018790535)
XLA Ops:
  0.0 0.0 copy-start
  0.8 0.7 copy-done
  1.5 0.5 collective-permute-start.2
  2.0 0.1 collective-permute-start
  2.0 0.5 collective-permute-start.1
  2.5 0.1 collective-permute-start.3
  2.5 1.3 %collective-permute-done.3.other_fresh = s32[1,2,16]{2,1,0:T(2,128)S(1)} collective-permute-done((s32[1,2,16]{2,1,0:T(2,128)}, s32[1,2,16]{2,1,0:T(2,128)S(1)}, u32[]{:S(2)}, u32[]{:S(2)}) %collective-permute-start.3) | collective-permute-done | bytes 160 | tf_op jit(solution)/shard_map/ppermute | solution.py:433
  3.8 0.0 collective-permute-done.2.other_mod
  3.8 0.0 collective-permute-done.other_keys
  3.8 0.0 collective-permute-done.1.other_values
  3.9 0.3 collective-permute-start.4
  4.1 0.3 collective-permute-start.5
  4.4 1.7 %shard_map.91 = (bf16[16,4,3072]{2,1,0:T(4,128)(2,1)S(1)}, bf16[256,3072]{1,0:T(8,128)(2,1)S(1)}) custom-call(bf16[3,2,3072]{2,1,0:T(2,128)(2,1)} %bitcast.29, bf16[3,2,3072]{2,1,0:T(2,128)(2,1)} %bitcast.31, bf16[3,2,3072]{2,1,0:T(2,128)(2,1)} %bitcast.33, bf16[3,2,3072]{2,1,0:T(2,128)(2,1)S(1)} %collective-permute-done.other_keys, ...), custom_call_target="tpu_custom_call" | custom-call | bytes 1000000 | tf_op jit(solution)/shard_map/pallas_call | solution.py:135
  6.1 20.5 %all_to_all.25.arrived = bf16[16,4,3072]{2,1,0:T(4,128)(2,1)S(1)} all-to-all(bf16[16,4,3072]{2,1,0:T(4,128)(2,1)S(1)} %get-tuple-element.27), channel_id=1, replica_groups=mesh['section'=2,'blk'=16] {'blk'}, dimensions={0} | all-to-all | bytes 786432 | tf_op jit(solution)/shard_map/all_to_all | solution.py:429
  26.7 0.0 collective-permute-done.5.other_out.other
  26.7 0.0 collective-permute-done.4.other
  26.7 0.0 copy-start.3
  26.7 0.0 copy-start.4
  26.7 3.3 %shard_map.92 = (bf16[72,128]{1,0:T(8,128)(2,1)S(1)}, bf16[72,128]{1,0:T(8,128)(2,1)S(1)}, bf16[72,128]{1,0:T(8,128)(2,1)S(1)}, bf16[48,192]{1,0:T(8,128)(2,1)S(1)}) custom-call(bf16[16,4,3072]{2,1,0:T(4,128)(2,1)S(1)} %all_to_all.25.arrived, bf16[256,3072]{1,0:T(8,128)(2,1)S(1)} %get-tuple-element.28.early, bf16[576,3072]{1,0:T(8,128)(2,1)} %bitcast.24, ...), custom_call_target="tpu_custom_call" | custom-call | flops 169869312 | bytes 4718592 | tf_op jit(solution)/shard_map/pallas_call | solution.py:135
  30.0 0.0 copy-start.2
  30.0 0.8 collective-permute-start.6
  30.8 2.2 %collective-permute-start.7 = (bf16[72,128]{1,0:T(8,128)(2,1)S(1)}, bf16[72,128]{1,0:T(8,128)(2,1)S(1)}, u32[]{:S(2)}, u32[]{:S(2)}) collective-permute-start(bf16[72,128]{1,0:T(8,128)(2,1)S(1)} %get-tuple-element.35), channel_id=1, source_target_pairs={{0,6},{1,7},{2,8},{3,9},{4,10},{5,11},{6,12},{7,13},{8,14},{9,15},... | collective-permute-start | bytes 55304 | tf_op jit(solution)/shard_map/ppermute | solution.py:439
  32.9 0.1 shard_map.93.old
  33.1 1.6 %collective-permute-done.6.chunk1 = bf16[72,128]{1,0:T(8,128)(2,1)S(1)} collective-permute-done((bf16[72,128]{1,0:T(8,128)(2,1)S(1)}, bf16[72,128]{1,0:T(8,128)(2,1)S(1)}, u32[]{:S(2)}, u32[]{:S(2)}) %collective-permute-start.6) | collective-permute-done | bytes 18464 | tf_op jit(solution)/shard_map/ppermute | solution.py:439
  34.7 1.7 %collective-permute-done.7.chunk2 = bf16[72,128]{1,0:T(8,128)(2,1)S(1)} collective-permute-done((bf16[72,128]{1,0:T(8,128)(2,1)S(1)}, bf16[72,128]{1,0:T(8,128)(2,1)S(1)}, u32[]{:S(2)}, u32[]{:S(2)}) %collective-permute-start.7) | collective-permute-done | bytes 18464 | tf_op jit(solution)/shard_map/ppermute | solution.py:439
  36.4 0.0 copy-done.3
  36.4 0.0 copy-done.4
  36.4 1.3 %shard_map.94 = bf16[16,72,128]{2,1,0:T(8,128)(2,1)S(1)} custom-call(bf16[72,128]{1,0:T(8,128)(2,1)S(1)} %get-tuple-element.32.chunk0, bf16[72,128]{1,0:T(8,128)(2,1)S(1)} %collective-permute-done.6.chunk1, bf16[72,128]{1,0:T(8,128)(2,1)S(1)} %collective-permute-done.7.chunk2, bf16[2,48,384]{2,1,0:T(8,128)(2,1)S(1)} %shard_map.93.old, ...), custom_call_target="tpu_custom_call" | custom-call | flops 3538944 | bytes 300000 | tf_op jit(solution)/shard_map/pallas_call | solution.py:135
  37.7 0.0 copy-start.1
  37.7 14.0 %all_to_all.26.blocks = bf16[16,72,128]{2,1,0:T(8,128)(2,1)S(1)} all-to-all(bf16[16,72,128]{2,1,0:T(8,128)(2,1)S(1)} %shard_map.94), channel_id=1, replica_groups=mesh['section'=2,'blk'=16] {'blk'}, dimensions={0} | all-to-all | bytes 589824 | tf_op jit(solution)/shard_map/all_to_all | solution.py:429
  51.6 0.0 copy-done.2
  51.6 0.9 shard_map.95
  52.5 12.4 %all_to_all.27.blocks = bf16[16,72,128]{2,1,0:T(8,128)(2,1)S(1)} all-to-all(bf16[16,72,128]{2,1,0:T(8,128)(2,1)S(1)} %get-tuple-element.39), channel_id=1, replica_groups=mesh['section'=2,'blk'=16] {'blk'}, dimensions={0} | all-to-all | bytes 589824 | tf_op jit(solution)/shard_map/all_to_all | solution.py:429
  64.9 0.0 copy-done.1
  64.9 1.7 %shard_map.96 = (bf16[72,128]{1,0:T(8,128)(2,1)S(1)}, bf16[72,128]{1,0:T(8,128)(2,1)S(1)}, bf16[72,128]{1,0:T(8,128)(2,1)S(1)}, bf16[48,192]{1,0:T(8,128)(2,1)S(1)}) custom-call(bf16[16,72,128]{2,1,0:T(8,128)(2,1)S(1)} %all_to_all.27.blocks, bf16[576,3072]{1,0:T(8,128)(2,1)S(1)} %bitcast.25, bf16[576,3072]{1,0:T(8,128)(2,1)S(1)} %collective-permute-done.4.other, ...), custom_call_target="tpu_custom_call" | custom-call | flops 169869312 | bytes 4718592 | tf_op jit(solution)/shard_map/pallas_call | solution.py:135
  66.6 1.3 %collective-permute-start.8 = (bf16[72,128]{1,0:T(8,128)(2,1)S(1)}, bf16[72,128]{1,0:T(8,128)(2,1)S(1)}, u32[]{:S(2)}, u32[]{:S(2)}) collective-permute-start(bf16[72,128]{1,0:T(8,128)(2,1)S(1)} %get-tuple-element.41), channel_id=1, source_target_pairs={{0,11},{1,12},{2,13},{3,14},{4,15},{5,0},{6,1},{7,2},{8,3},{9,4},{... | collective-permute-start | bytes 55304 | tf_op jit(solution)/shard_map/ppermute | solution.py:439
  67.9 2.6 %collective-permute-start.9 = (bf16[72,128]{1,0:T(8,128)(2,1)S(1)}, bf16[72,128]{1,0:T(8,128)(2,1)S(1)}, u32[]{:S(2)}, u32[]{:S(2)}) collective-permute-start(bf16[72,128]{1,0:T(8,128)(2,1)S(1)} %get-tuple-element.42), channel_id=1, source_target_pairs={{0,6},{1,7},{2,8},{3,9},{4,10},{5,11},{6,12},{7,13},{8,14},{9,15},... | collective-permute-start | bytes 55304 | tf_op jit(solution)/shard_map/ppermute | solution.py:439
  70.4 0.8 collective-permute-done.8.chunk1
  71.3 2.2 %collective-permute-done.9.chunk2 = bf16[72,128]{1,0:T(8,128)(2,1)S(1)} collective-permute-done((bf16[72,128]{1,0:T(8,128)(2,1)S(1)}, bf16[72,128]{1,0:T(8,128)(2,1)S(1)}, u32[]{:S(2)}, u32[]{:S(2)}) %collective-permute-start.9) | collective-permute-done | bytes 18464 | tf_op jit(solution)/shard_map/ppermute | solution.py:439
  73.4 1.3 %shard_map.97 = bf16[16,72,128]{2,1,0:T(8,128)(2,1)S(1)} custom-call(bf16[72,128]{1,0:T(8,128)(2,1)S(1)} %get-tuple-element.40.chunk0, bf16[72,128]{1,0:T(8,128)(2,1)S(1)} %collective-permute-done.8.chunk1, bf16[72,128]{1,0:T(8,128)(2,1)S(1)} %collective-permute-done.9.chunk2, bf16[2,48,384]{2,1,0:T(8,128)(2,1)S(1)} %shard_map.93.old, ...), custom_call_target="tpu_custom_call" | custom-call | flops 3538944 | bytes 300000 | tf_op jit(solution)/shard_map/pallas_call | solution.py:135
  74.7 13.2 %all_to_all.28.blocks = bf16[16,72,128]{2,1,0:T(8,128)(2,1)S(1)} all-to-all(bf16[16,72,128]{2,1,0:T(8,128)(2,1)S(1)} %shard_map.97), channel_id=1, replica_groups=mesh['section'=2,'blk'=16] {'blk'}, dimensions={0} | all-to-all | bytes 589824 | tf_op jit(solution)/shard_map/all_to_all | solution.py:429
  88.0 0.7 shard_map.98
  88.7 9.7 %all_to_all.29.arrived = bf16[32,4,192]{2,1,0:T(4,128)(2,1)S(1)} all-to-all(bf16[32,4,192]{2,1,0:T(4,128)(2,1)S(1)} %shard_map.98), channel_id=1, replica_groups=mesh['section'=2,'blk'=16] {'section','blk'}, dimensions={0} | all-to-all | bytes 98304 | tf_op jit(solution)/shard_map/all_to_all | solution.py:429
  98.4 0.8 shard_map.99
  (1 shorter events, 0.0 us)
Async XLA Ops:
  0.0 1.5 %copy-start = (f32[1,50,3,3072]{3,0,2,1:T(1,128)S(1)}, f32[1,50,3,3072]{3,0,2,1:T(1,128)}, u32[]{:S(2)}) copy-start(f32[1,50,3,3072]{3,0,2,1:T(1,128)} %param.12) | copy-start | bytes 5529604
  1.5 2.3 %collective-permute-start.2 = (f32[3,1,3072]{2,1,0:T(1,128)S(1)}, f32[3,1,3072]{2,1,0:T(1,128)S(1)}, u32[]{:S(2)}, u32[]{:S(2)}) collective-permute-start(f32[3,1,3072]{2,1,0:T(1,128)S(1)} %dynamic-slice_bitcast_fusion.mod), channel_id=1, source_target_pairs={{0,16},{16,0},{1,17},{17,1},{2,18},{18,2},{3,19},{19,3},{4,20},{20... | collective-permute-start | bytes 110600 | tf_op jit(solution)/shard_map/ppermute | solution.py:433
  2.0 1.9 %collective-permute-start = (bf16[3,2,3072]{2,1,0:T(2,128)(2,1)}, bf16[3,2,3072]{2,1,0:T(2,128)(2,1)S(1)}, u32[]{:S(2)}, u32[]{:S(2)}) collective-permute-start(bf16[3,2,3072]{2,1,0:T(2,128)(2,1)} %bitcast.30), channel_id=1, source_target_pairs={{0,16},{16,0},{1,17},{17,1},{2,18},{18,2},{3,19},{19,3},{4,20},{20... | collective-permute-start | bytes 110600 | tf_op jit(solution)/shard_map/ppermute | solution.py:433
  2.0 1.8 %collective-permute-start.1 = (bf16[3,2,3072]{2,1,0:T(2,128)(2,1)}, bf16[3,2,3072]{2,1,0:T(2,128)(2,1)S(1)}, u32[]{:S(2)}, u32[]{:S(2)}) collective-permute-start(bf16[3,2,3072]{2,1,0:T(2,128)(2,1)} %bitcast.32), channel_id=1, source_target_pairs={{0,16},{16,0},{1,17},{17,1},{2,18},{18,2},{3,19},{19,3},{4,20},{20... | collective-permute-start | bytes 110600 | tf_op jit(solution)/shard_map/ppermute | solution.py:433
  2.5 1.4 %collective-permute-start.3 = (s32[1,2,16]{2,1,0:T(2,128)}, s32[1,2,16]{2,1,0:T(2,128)S(1)}, u32[]{:S(2)}, u32[]{:S(2)}) collective-permute-start(s32[1,2,16]{2,1,0:T(2,128)} %fresh.3), channel_id=1, source_target_pairs={{0,16},{16,0},{1,17},{17,1},{2,18},{18,2},{3,19},{19,3},{4,20},{20... | collective-permute-start | bytes 392 | tf_op jit(solution)/shard_map/ppermute | solution.py:433
  3.9 22.8 %collective-permute-start.4 = (bf16[576,3072]{1,0:T(8,128)(2,1)}, bf16[576,3072]{1,0:T(8,128)(2,1)S(1)}, u32[]{:S(2)}, u32[]{:S(2)}) collective-permute-start(bf16[576,3072]{1,0:T(8,128)(2,1)} %bitcast.22), channel_id=1, source_target_pairs={{0,16},{16,0},{1,17},{17,1},{2,18},{18,2},{3,19},{19,3},{4,20},{20... | collective-permute-start | bytes 10616840 | tf_op jit(solution)/shard_map/ppermute | solution.py:433
  4.1 22.6 %collective-permute-start.5 = (bf16[192,3072]{1,0:T(8,128)(2,1)}, bf16[192,3072]{1,0:T(8,128)(2,1)S(1)}, u32[]{:S(2)}, u32[]{:S(2)}) collective-permute-start(bf16[192,3072]{1,0:T(8,128)(2,1)} %bitcast.26), channel_id=1, source_target_pairs={{0,16},{16,0},{1,17},{17,1},{2,18},{18,2},{3,19},{19,3},{4,20},{20... | collective-permute-start | bytes 3538952 | tf_op jit(solution)/shard_map/ppermute | solution.py:433
  26.7 9.7 %copy-start.3 = (s32[1,2,16]{2,1,0:T(2,128)S(1)}, s32[1,2,16]{2,1,0:T(2,128)}, u32[]{:S(2)}) copy-start(s32[1,2,16]{2,1,0:T(2,128)} %fresh.3) | copy-start | bytes 388
  26.7 9.7 %copy-start.4 = (s32[2,16]{1,0:T(2,128)S(1)}, s32[2,16]{1,0:T(2,128)}, u32[]{:S(2)}) copy-start(s32[2,16]{1,0:T(2,128)} %live.3) | copy-start | bytes 388
  30.0 21.7 %copy-start.2 = (bf16[1,3072,192]{1,2,0:T(8,128)(2,1)S(1)}, bf16[1,3072,192]{1,2,0:T(8,128)(2,1)}, u32[]{:S(2)}) copy-start(bf16[1,3072,192]{1,2,0:T(8,128)(2,1)} %param.11) | copy-start | bytes 3538948
  30.0 4.7 %collective-permute-start.6 = (bf16[72,128]{1,0:T(8,128)(2,1)S(1)}, bf16[72,128]{1,0:T(8,128)(2,1)S(1)}, u32[]{:S(2)}, u32[]{:S(2)}) collective-permute-start(bf16[72,128]{1,0:T(8,128)(2,1)S(1)} %get-tuple-element.34), channel_id=1, source_target_pairs={{0,11},{1,12},{2,13},{3,14},{4,15},{5,0},{6,1},{7,2},{8,3},{9,4},{... | collective-permute-start | bytes 55304 | tf_op jit(solution)/shard_map/ppermute | solution.py:439
  30.8 5.6 %collective-permute-start.7 = (bf16[72,128]{1,0:T(8,128)(2,1)S(1)}, bf16[72,128]{1,0:T(8,128)(2,1)S(1)}, u32[]{:S(2)}, u32[]{:S(2)}) collective-permute-start(bf16[72,128]{1,0:T(8,128)(2,1)S(1)} %get-tuple-element.35), channel_id=1, source_target_pairs={{0,6},{1,7},{2,8},{3,9},{4,10},{5,11},{6,12},{7,13},{8,14},{9,15},... | collective-permute-start | bytes 55304 | tf_op jit(solution)/shard_map/ppermute | solution.py:439
  37.7 27.2 %copy-start.1 = (bf16[1,3072,576]{1,2,0:T(8,128)(2,1)S(1)}, bf16[1,3072,576]{1,2,0:T(8,128)(2,1)}, u32[]{:S(2)}) copy-start(bf16[1,3072,576]{1,2,0:T(8,128)(2,1)} %param.10) | copy-start | bytes 10616836
  66.6 4.7 %collective-permute-start.8 = (bf16[72,128]{1,0:T(8,128)(2,1)S(1)}, bf16[72,128]{1,0:T(8,128)(2,1)S(1)}, u32[]{:S(2)}, u32[]{:S(2)}) collective-permute-start(bf16[72,128]{1,0:T(8,128)(2,1)S(1)} %get-tuple-element.41), channel_id=1, source_target_pairs={{0,11},{1,12},{2,13},{3,14},{4,15},{5,0},{6,1},{7,2},{8,3},{9,4},{... | collective-permute-start | bytes 55304 | tf_op jit(solution)/shard_map/ppermute | solution.py:439
  67.9 5.6 %collective-permute-start.9 = (bf16[72,128]{1,0:T(8,128)(2,1)S(1)}, bf16[72,128]{1,0:T(8,128)(2,1)S(1)}, u32[]{:S(2)}, u32[]{:S(2)}) collective-permute-start(bf16[72,128]{1,0:T(8,128)(2,1)S(1)} %get-tuple-element.42), channel_id=1, source_target_pairs={{0,6},{1,7},{2,8},{3,9},{4,10},{5,11},{6,12},{7,13},{8,14},{9,15},... | collective-permute-start | bytes 55304 | tf_op jit(solution)/shard_map/ppermute | solution.py:439
